TPU v7x, 256 devices: a whole 4x4x8 slice. The times are simulated.
256 devices in a mesh: seq: 64 (over z, y, core), head: 4 (over x).
Axes of the slice: x: 4, y: 4, z: 8, core: 2. Of those that a mesh axis runs over, the one named last changes fastest.
Arguments:
- queries: bfloat16 [6, 8, 128, 128], P(None, None, 'head'), may hold values from -16 to 16
- key_cache: bfloat16 [6, 122880, 8, 128], P(None, 'seq', 'head'), may hold values from -16 to 16
- value_cache: bfloat16 [6, 122880, 8, 128], P(None, 'seq', 'head'), may hold values from -12 to 12
- grad_out: bfloat16 [6, 8, 128, 128], P(None, None, 'head'), may hold values from -20 to 20
- cache_len: int32 [6], replicated, may hold values from 61440 to 122880, as said below
Outputs:
- grad_queries: bfloat16 [6, 8, 128, 128], P(None, None, 'head')
Inputs may be any that keep to these rules, and one draw needn't show every extreme that they name: The 8 queries of sequence b stand at positions cache_len[b] - 8 to cache_len[b] - 1 of its cache. Some sequence has all 122880 positions valid.
All inputs are finite; a program needn't handle non-finite values.
Results may differ from a plain program's by a relative error of at most 0.0058.
Values may be sent and summed in bfloat16 or wider, within the bound.
No kernel may reach another device: no remote copies, remote signals or barrier semaphores. Data moves between devices by JAX's collectives and lax.ppermute only.
A program may use at most 128 MiB of HBM per device.

v0:
```python
import math

import jax
import jax.numpy as jnp
from jax import lax
from jax.sharding import PartitionSpec as P

B = 6
QT = 8
HQ = 128
HD = 128


NEGATIVE = -1e30
EPSILON = 1e-06


def joined(part, axis, combine):
    gathered = jax.tree.map(lambda a: lax.all_gather(a, axis), part)

    def take(source):
        return jax.tree.map(lambda a: lax.dynamic_index_in_dim(a, source, 0, False), gathered)

    return lax.fori_loop(
        1, lax.axis_size(axis), lambda source, state: combine(state, take(source)), take(0)
    )


def combine_stats(left_stats, right_stats):
    left_max, left_total, left_dot = left_stats
    right_max, right_total, right_dot = right_stats
    largest = jnp.maximum(left_max, right_max)
    left_factor = jnp.exp(left_max - largest)
    right_factor = jnp.exp(right_max - largest)
    merged_total = left_total * left_factor + right_total * right_factor
    merged_dot = left_dot * left_factor + right_dot * right_factor
    return (largest, merged_total, merged_dot)


def local(queries, key_cache, value_cache, grad_out, cache_len):
    seq_count, query_count, head_count, head_width = queries.shape
    cache_span = key_cache.shape[1]
    kv_count = key_cache.shape[2]
    groups = head_count // kv_count
    score_scale = 1.0 / math.sqrt(head_width)
    query_groups = queries.reshape(seq_count, query_count, kv_count, groups, head_width)
    grad_groups = grad_out.reshape(seq_count, query_count, kv_count, groups, head_width)
    scores = (
        jnp.einsum("btgih,bsgh->bgtis", query_groups, key_cache, preferred_element_type=jnp.float32)
        * score_scale
    )
    offset = lax.axis_index("seq") * cache_span
    key_index = offset + jnp.arange(cache_span, dtype=jnp.int32)
    key_limit = cache_len[:, None] - query_count + jnp.arange(query_count, dtype=jnp.int32)[None, :]
    visible = key_index[None, None, None, None, :] <= key_limit[:, None, :, None, None]
    masked = jnp.where(visible, scores, NEGATIVE)
    local_max = jnp.max(masked, axis=4)
    local_weights = jnp.where(visible, jnp.exp(masked - local_max[..., None]), 0.0)
    local_total = jnp.sum(local_weights, axis=4)
    grad_prob = jnp.einsum(
        "btgih,bsgh->bgtis", grad_groups, value_cache, preferred_element_type=jnp.float32
    )
    local_dot = jnp.sum(local_weights * grad_prob, axis=4)
    row_max, softmax_total, dot_total = joined(
        (local_max, local_total, local_dot), "seq", combine_stats
    )
    out_dot = dot_total / softmax_total
    softmax_prob = local_weights * (jnp.exp(local_max - row_max) / softmax_total)[..., None]
    grad_score = (softmax_prob * (grad_prob - out_dot[..., None])).astype(jnp.bfloat16)
    grad_part = (
        jnp.einsum("bgtis,bsgh->btgih", grad_score, key_cache, preferred_element_type=jnp.float32)
        * score_scale
    )
    grad_part = grad_part.reshape(seq_count, query_count, head_count, head_width)
    entry_count = B * QT * HQ * HD
    grad_sum = lax.psum(grad_part, "seq")
    squares = lax.psum(jnp.sum(grad_sum * grad_sum), "head")
    norm_scale = jnp.sqrt(squares / entry_count + EPSILON)
    return (grad_sum / norm_scale).astype(jnp.bfloat16)


def solution(mesh):
    placed = (
        P(None, None, "head", None),
        P(None, "seq", "head", None),
        P(None, "seq", "head", None),
        P(None, None, "head", None),
        P(),
    )
    return jax.shard_map(
        local, mesh=mesh, in_specs=placed, out_specs=P(None, None, "head", None), check_vma=False
    )
```

profile of v0, /device:TPU:1, one launch (start us, length us, event | category | flops | bytes accessed | tf_op | source)
XLA Modules:
  0.0 511.3 jit_solution(5760362864459603054)
XLA Ops:
  7.4 10.3 %fusion.3 = (f32[6,2,8,16]{3,2,1,0:T(8,128)S(1)}, f32[6,2,8,16,1920]{4,3,2,1,0:T(8,128)}) fusion(pred[6,8,1920]{2,1,0:T(8,128)(4,1)S(1)} %broadcast_compare_fusion, bf16[6,1920,2,128,1]{3,2,1,0,4:T(2,128)(2,1)} %bitcast.35, bf16[6,8,2,16,128]{4,3,2,1,0:T(8,128)(2,1)} %bitcast.41), kind=kOutput, calls=%fused_computation.12 | convolution fusion | flops 763820544 | bytes 18186240 | tf_op jit(solution)/shard_map/btgih,bsgh->bgtis/dot_general | solution.py:49
  17.7 56.6 %all-gather = f32[384,2,8,16]{3,2,1,0:T(8,128)S(1)} all-gather(f32[6,2,8,16]{3,2,1,0:T(8,128)S(1)} %get-tuple-element.206), channel_id=2, replica_groups=mesh['seq'=64,'head'=4] {'seq'}, dimensions={0}, use_global_device_ids=true | all-gather | bytes 399360 | tf_op jit(solution)/shard_map/all_gather | solution.py:19
  74.4 12.9 %multiply_reduce_fusion = (f32[6,2,8,16]{3,2,1,0:T(8,128)S(1)}, f32[6,2,8,16]{3,2,1,0:T(8,128)S(1)}, f32[6,2,8,16,1920]{4,3,2,1,0:T(8,128)}) fusion(f32[6,2,8,16]{3,2,1,0:T(8,128)S(1)} %get-tuple-element.206, f32[6,2,8,16,1920]{4,3,2,1,0:T(8,128)} %get-tuple-element.207, pred[6,8,1920]{2,1,0:T(8,128)(4,1)S(1)} %broadcast_compare_fusion, ...), kind=kOutput, calls=%fused_computation.9 | convolution fusion | flops 775615488 | bytes 29995008 | tf_op jit(solution)/shard_map/btgih,bsgh->bgtis/dot_general | solution.py:60
  87.2 50.9 %all-gather.2 = f32[384,2,8,16]{3,2,1,0:T(8,128)S(1)} all-gather(f32[6,2,8,16]{3,2,1,0:T(8,128)S(1)} %get-tuple-element.186), channel_id=4, replica_groups=mesh['seq'=64,'head'=4] {'seq'}, dimensions={0}, use_global_device_ids=true | all-gather | bytes 399360 | tf_op jit(solution)/shard_map/all_gather | solution.py:19
  138.1 49.8 %all-gather.1 = f32[384,2,8,16]{3,2,1,0:T(8,128)S(1)} all-gather(f32[6,2,8,16]{3,2,1,0:T(8,128)S(1)} %get-tuple-element.187), channel_id=3, replica_groups=mesh['seq'=64,'head'=4] {'seq'}, dimensions={0}, use_global_device_ids=true | all-gather | bytes 399360 | tf_op jit(solution)/shard_map/all_gather | solution.py:19
  187.9 1.7 copy-done.1
  189.6 108.2 %while.19 = (s32[]{:T(128)}, f32[6,2,8,16]{3,2,1,0:T(8,128)S(1)}, f32[6,2,8,16]{3,2,1,0:T(8,128)S(1)}, f32[6,2,8,16]{3,2,1,0:T(8,128)S(1)}, f32[64,6,2,8,16]{4,3...) while((s32[]{:T(128)}, f32[6,2,8,16]{3,2,1,0:T(8,128)S(1)}, ...), condition=%wide.region_4.5_spmd, body=%wide.region_3.4_spmd.sunk | while | flops 16901 | bytes 86159 | solution.py:24
  190.5 0.8 fusion.27
  192.2 0.8 fusion.27
  193.9 0.8 fusion.27
  195.6 0.8 fusion.27
  197.3 0.8 fusion.27
  199.0 0.8 fusion.27
  200.8 0.8 fusion.27
  202.5 0.8 fusion.27
  219.7 0.8 fusion.27
  221.4 0.8 fusion.27
  223.1 0.8 fusion.27
  297.9 12.5 %fusion.16 = f32[6,8,2,16,128]{4,3,1,2,0:T(8,128)S(1)} fusion(bf16[6,1920,2,128,1]{3,2,1,0,4:T(2,128)(2,1)} %bitcast.36, f32[6,2,8,16,1920]{4,3,2,1,0:T(8,128)} %get-tuple-element.208, f32[6,2,8,16]{3,2,1,0:T(8,128)S(1)} %get-tuple-element.205, f32[6,2,8,16]{3,2,1,0:T(8,128)S(1)} %get-tuple-element.204, f32[6,2,8,16]{3,2,1,0:T(8,128)S(1)} %get-tuple-element.206, ...), kind=kOutput, calls=%fused_computation.23 | convolution fusion | flops 778764288 | bytes 30388224 | tf_op jit(solution)/shard_map/bgtis,bsgh->btgih/dot_general | solution.py:71
  310.4 1.0 copy.22
  311.4 179.4 %all-reduce.2.cloned.1.call-done = f32[6,8,32,128]{3,2,1,0:T(8,128)} async-done(((f32[6,8,32,128]{3,2,1,0:T(8,128)}), f32[6,8,32,128]{3,2,1,0:T(8,128)}) %all-reduce.2.cloned.1.call-update) | async-done | bytes 786448 | tf_op jit(solution)/shard_map/psum | solution.py:76
  490.8 1.9 multiply_reduce_fusion.1
  492.8 9.0 %psum.15 = f32[]{:T(128)} all-reduce(f32[]{:T(128)} %multiply_reduce_fusion.1), channel_id=1, replica_groups=mesh['seq'=64,'head'=4] {'head'}, use_global_device_ids=true, to_apply=%region_7.8 | all-reduce | flops 1 | bytes 8 | tf_op jit(solution)/shard_map/psum | solution.py:77
  502.5 2.0 divide_convert_fusion
  (195 shorter events, 98.1 us)
Async XLA Ops:
  6.5 484.3 %all-reduce.2.cloned.1.call-start = ((), (), s32[]{:S(2)}) async-start(), calls=%async_computation | async-start | bytes 1572864 | tf_op jit(solution)/shard_map/psum | solution.py:76
  7.4 66.9 %copy-start.2 = (bf16[6,1920,2,128]{3,2,1,0:T(2,128)(2,1)S(1)}, bf16[6,1920,2,128]{3,2,1,0:T(2,128)(2,1)}, u32[]{:S(2)}) copy-start(bf16[6,1920,2,128]{3,2,1,0:T(2,128)(2,1)} %param.9) | copy-start | bytes 17694724
  7.4 66.9 %copy-start.3 = (bf16[6,8,32,128]{3,2,1,0:T(8,128)(2,1)S(1)}, bf16[6,8,32,128]{3,2,1,0:T(8,128)(2,1)}, u32[]{:S(2)}) copy-start(bf16[6,8,32,128]{3,2,1,0:T(8,128)(2,1)} %param.10) | copy-start | bytes 1179652
  138.1 49.8 %copy-start = (f32[384,2,8,16]{3,2,1,0:T(8,128)}, f32[384,2,8,16]{3,2,1,0:T(8,128)S(1)}, u32[]{:S(2)}) copy-start(f32[384,2,8,16]{3,2,1,0:T(8,128)S(1)} %all-gather.2) | copy-start | bytes 1179652
  187.9 1.7 copy-start.1
Sparse Core Ops, SparseCore 0:
  311.6 179.2 all-reduce.1
where the time goes:
time: 521 us; the launch traced here: 511 us
  waiting for transfers between devices  179 us (34%)
  blocking collectives  166 us (32%)
  other arithmetic  111 us (21%)
  matrix products  35.6 us (7%)
  between operations  14.2 us (3%)
    psum x1, waiting for transfers between devices, local(): grad_sum = lax.psum(grad_part, 'seq')  179 us
    all_gather x3, blocking collectives, joined(): gathered = jax.tree.map(lambda a: lax.all_gather(a, axis), part)  157 us
    add x63, other arithmetic, combine_stats(): merged_total = left_total * left_factor + right_total * right_factor  53.2 us
    add x63, other arithmetic, combine_stats(): merged_dot = left_dot * left_factor + right_dot * right_factor  52.9 us
    dot_general x1, matrix products, local(): jnp.einsum('btgih,bsgh->bgtis', grad_groups, value_cache, preferred_eleme...  12.9 us
    dot_general x1, matrix products, local(): jnp.einsum('bgtis,bsgh->btgih', grad_score, key_cache, preferred_element_...  12.5 us
  transfers between devices with their start and end apart: 1, of which 1 were waited for; matrix products, arithmetic and copies ran while one was open for 0% of the time, Pallas kernels for 0%

commit v1 on v0

v1 whole, which is shorter than its diff:
```python
import math

import jax
import jax.numpy as jnp
from jax import lax
from jax.experimental import pallas as pl
from jax.experimental.pallas import tpu as pltpu
from jax.sharding import Mesh
from jax.sharding import PartitionSpec as P

B = 6
QT = 8
HQ = 128
HD = 128

NEGATIVE = -1e30
FLOOR = -1e29
EPSILON = 1e-06
SCALE = 1.0 / math.sqrt(HD)
SCALE2 = SCALE * math.log2(math.e)
CHUNK = 256
TILES = CHUNK // 8
PARTS = 3
SLOT = 56
MIB = 1024 * 1024
VMEM = pl.BlockSpec(memory_space=pltpu.VMEM)
HBM = pl.BlockSpec(memory_space=pltpu.HBM)
FIRST = (((0,), (0,)), ((), ()))


def high(x):
    return x.astype(jnp.bfloat16).astype(jnp.float32)


def attend(
    len_ref, q_hbm, k_hbm, v_hbm, go_hbm, peer_ref, own_ref, own_st_ref,
    q_buf, go_buf, k_buf, v_buf, s_a, s_b, s_c, g_a, g_b, g_c, sems,
):
    core = lax.axis_index("c")
    count, rows = k_buf.shape[0], k_buf.shape[1]
    span = rows // 2
    chunks = rows // CHUNK
    start = ((lax.axis_index("z") * 4 + lax.axis_index("y")) * 2 + core) * span

    def sequence(j):
        return 2 * j + 1 - core if j < PARTS else 2 * (j - PARTS) + core

    small = [
        pltpu.make_async_copy(q_hbm, q_buf, sems.at[2 * count]),
        pltpu.make_async_copy(go_hbm, go_buf, sems.at[2 * count + 1]),
    ]
    keys = [pltpu.make_async_copy(k_hbm.at[sequence(j)], k_buf.at[j], sems.at[2 * j]) for j in range(count)]
    values = [pltpu.make_async_copy(v_hbm.at[sequence(j)], v_buf.at[j], sems.at[2 * j + 1]) for j in range(count)]
    small[0].start()
    keys[0].start()
    small[1].start()
    values[0].start()
    for j in range(1, count):
        keys[j].start()
        values[j].start()

    scores, probs = (s_a, s_b, s_c), (g_a, g_b, g_c)
    even8 = lax.broadcasted_iota(jnp.int32, (8, 128), 0) % 2 == 0
    odd_row = lax.broadcasted_iota(jnp.int32, (CHUNK, 128), 0) % 2 == 1
    keep_odd = odd_row.astype(jnp.float32).astype(jnp.bfloat16)
    keep_even = (1.0 - odd_row.astype(jnp.float32)).astype(jnp.bfloat16)
    lead = lax.broadcasted_iota(jnp.int32, (8, 128), 1) // 16 - lax.broadcasted_iota(jnp.int32, (8, 128), 0) // 2
    tile_start = lax.broadcasted_iota(jnp.int32, (TILES, 8, 128), 0) * 4

    def turned(x):
        both = jnp.concatenate([x[:, :16].reshape(128, HD), x[:, 16:].reshape(128, HD)], axis=0)
        return both.T

    def sides(x, reduce, fill):
        return (
            reduce(jnp.where(even8, x, fill), axis=0, keepdims=True),
            reduce(jnp.where(even8, fill, x), axis=0, keepdims=True),
        )

    def score_step(j, i, qt, gt, room, top):
        at = slice(i * CHUNK, (i + 1) * CHUNK)
        s = jnp.dot(k_buf[j, at, :], qt, preferred_element_type=jnp.float32)
        s = jnp.where(odd_row, s[:, 128:], s[:, :128]).reshape(TILES, 8, 128)
        s = jnp.where((room + lead - i * (CHUNK // 2))[None] >= tile_start, s, NEGATIVE)
        scores[j % 3][at, :] = s.reshape(CHUNK, 128)
        g = jnp.dot(v_buf[j, at, :], gt, preferred_element_type=jnp.float32)
        probs[j % 3][at, :] = jnp.where(odd_row, g[:, 128:], g[:, :128])
        return jnp.maximum(top, jnp.max(s, axis=0))

    def weight_step(j, i, tops, total, dot):
        at = slice(i * CHUNK, (i + 1) * CHUNK)
        s = scores[j % 3][at, :].reshape(TILES, 8, 128)
        w = jnp.exp2((s - tops[None]) * SCALE2)
        scores[j % 3][at, :] = w.reshape(CHUNK, 128)
        wg = w * probs[j % 3][at, :].reshape(TILES, 8, 128)
        return total + jnp.sum(w, axis=0), dot + jnp.sum(wg, axis=0)

    def term_step(j, i, dots, acc):
        at = slice(i * CHUNK, (i + 1) * CHUNK)
        w = scores[j % 3][at, :].reshape(TILES, 8, 128)
        p = w * (probs[j % 3][at, :].reshape(TILES, 8, 128) - dots[None])
        pw = jnp.concatenate([p.reshape(CHUNK, 128), w.reshape(CHUNK, 128)], axis=1).astype(jnp.bfloat16)
        kc = k_buf[j, at, :]
        kk = jnp.concatenate([kc * keep_even, kc * keep_odd], axis=1)
        return acc + lax.dot_general(pw, kk, FIRST, preferred_element_type=jnp.float32)

    def prepare(j):
        seq = sequence(j)
        keys[j].wait()
        values[j].wait()
        return turned(q_buf[seq]), turned(go_buf[seq]), len_ref[seq] - QT - start

    def reference_of(top):
        return [high(jnp.maximum(m, FLOOR)) for m in sides(top, jnp.max, NEGATIVE)]

    def means_of(total, dot):
        totals = sides(total, jnp.sum, 0.0)
        dots = [
            jnp.where(t > 0.0, d / jnp.where(t > 0.0, t, 1.0), 0.0)
            for t, d in zip(totals, sides(dot, jnp.sum, 0.0))
        ]
        return totals, dots

    def store(j, acc, tops, totals, dots):
        pieces = []
        for half in (acc[:128], acc[128:]):
            pair = [half[:, side * 128 : (side + 1) * 128].reshape(8, 16, 128) for side in range(2)]
            pieces.append(jnp.concatenate(pair, axis=1).reshape(32, 8, 128))
        both = jnp.concatenate(pieces, axis=1)
        part = j % PARTS
        if j < PARTS:
            peer_ref[:, part * 16 : part * 16 + 16, :] = both.astype(jnp.bfloat16)
        else:
            own_ref[:, part * 16 : part * 16 + 16, :] = both
        sub = lax.broadcasted_iota(jnp.int32, (8, 128), 0)
        for side in range(2):
            if j < PARTS:
                t, d = totals[side], dots[side]
                cols = (tops[side], high(t), t - high(t), high(d), d - high(d))
            else:
                cols = (tops[side], totals[side], dots[side])
            block = jnp.zeros((8, 128), jnp.float32)
            for k, col in enumerate(cols):
                block = jnp.where(sub == k, col, block)
            blocks[j // PARTS, side, part] = block

    blocks = {}
    for copy in small:
        copy.wait()
    zero8 = jnp.zeros((8, 128), jnp.float32)
    stats = {}
    for n in range(count + 2):
        first, second, third = n, n - 1, n - 2
        if first < count:
            ready = prepare(first)
            top = jnp.full((8, 128), NEGATIVE, jnp.float32)
        if 0 <= second < count:
            tops = reference_of(last_top)
            tops8 = jnp.where(even8, *tops)
            total, dot = zero8, zero8
        if 0 <= third:
            dots8 = jnp.where(even8, *stats[third][2])
            acc = jnp.zeros((256, 256), jnp.float32)
        for i in range(chunks):
            if 0 <= third:
                acc = term_step(third, i, dots8, acc)
            if first < count:
                top = score_step(first, i, *ready, top)
            if 0 <= second < count:
                total, dot = weight_step(second, i, tops8, total, dot)
        if 0 <= third:
            store(third, acc, *stats[third])
        if 0 <= second < count:
            stats[second] = (tops, *means_of(total, dot))
        last_top = top

    blank = jnp.zeros((8, 128), jnp.float32)
    z = jnp.concatenate(
        [blocks.get((who, side, part), blank) for who in range(2) for side in range(2) for part in range(4)], axis=0
    ).T
    for who in range(2):
        pair = []
        for side in range(2):
            shift = (128 - who * 64 - side * 32) % 128
            pair.append((pltpu.roll(z, shift, 1) if shift else z).reshape(8, 16, 128))
        st = jnp.concatenate(pair, axis=1).reshape(32, 8, 128)
        if who == 0:
            peer_ref[:, 48:64, :] = jnp.concatenate([st, jnp.zeros_like(st)], axis=1).astype(jnp.bfloat16)
        else:
            own_st_ref[...] = st


def attend_call(lengths, q, k, v, go):
    count, span = k.shape[0], k.shape[1]
    k = k.reshape(count, span * 2, HD)
    v = v.reshape(count, span * 2, HD)
    wide = pltpu.VMEM((span * 2, 128), jnp.float32)
    return pl.pallas_call(
        attend,
        in_specs=[pl.BlockSpec(memory_space=pltpu.SMEM), HBM, HBM, HBM, HBM],
        out_specs=[VMEM, VMEM, VMEM],
        out_shape=[
            jax.ShapeDtypeStruct((32, 64, HD), jnp.bfloat16),
            jax.ShapeDtypeStruct((32, 48, HD), jnp.float32),
            jax.ShapeDtypeStruct((32, 8, HD), jnp.float32),
        ],
        scratch_shapes=[
            pltpu.VMEM(q.shape, jnp.bfloat16),
            pltpu.VMEM(go.shape, jnp.bfloat16),
            pltpu.VMEM(k.shape, jnp.bfloat16),
            pltpu.VMEM(v.shape, jnp.bfloat16),
            wide, wide, wide, wide, wide, wide,
            pltpu.SemaphoreType.DMA((2 * count + 2,)),
        ],
        compiler_params=pltpu.CompilerParams(vmem_limit_bytes=60 * MIB),
        cost_estimate=pl.CostEstimate(flops=4_500_000_000, bytes_accessed=14_000_000, transcendentals=3_000_000),
    )(lengths, q, k, v, go)


def column(st, part, k):
    at = 8 * part + k
    return st[:, :, at : at + 1]


def pair_up(peer_ref, own_ref, own_st_ref, out_ref):
    peer = peer_ref[...].astype(jnp.float32)
    own = own_ref[...]
    peer_st, own_st = peer[:, 48:56], own_st_ref[...]
    lane = lax.broadcasted_iota(jnp.int32, (32, 8, 128), 2)
    st = jnp.zeros((32, 8, 128), jnp.float32)
    pieces = []
    for part in range(PARTS):
        at = part * 16
        top_a, total_a, dot_a = (column(own_st, part, k) for k in range(3))
        top_b = column(peer_st, part, 0)
        total_b = column(peer_st, part, 1) + column(peer_st, part, 2)
        dot_b = column(peer_st, part, 3) + column(peer_st, part, 4)
        top = jnp.maximum(top_a, top_b)
        factor_a = jnp.exp2((top_a - top) * SCALE2)
        factor_b = jnp.exp2((top_b - top) * SCALE2)
        total_a, total_b = factor_a * total_a, factor_b * total_b
        total = total_a + total_b
        dot = (total_a * dot_a + total_b * dot_b) / jnp.where(total > 0.0, total, 1.0)
        term_a, term_b = own[:, at : at + 8], peer[:, at : at + 8]
        mass_a, mass_b = own[:, at + 8 : at + 16], peer[:, at + 8 : at + 16]
        pieces.append(
            factor_a * term_a + (factor_a * (dot_a - dot)) * mass_a
            + (factor_b * term_b + (factor_b * (dot_b - dot)) * mass_b)
        )
        pieces.append(factor_a * mass_a + factor_b * mass_b)
        for k, col in enumerate((top, high(total), total - high(total), high(dot), dot - high(dot))):
            st = jnp.where(lane == 8 * part + k, col, st)
    out_ref[...] = jnp.concatenate(pieces + [st], axis=1).astype(jnp.bfloat16)


def pair_up_call(peer, own, own_st):
    return pl.pallas_call(
        pair_up,
        in_specs=[VMEM] * 3,
        out_specs=VMEM,
        out_shape=jax.ShapeDtypeStruct((32, SLOT, HD), jnp.bfloat16),
        compiler_params=pltpu.CompilerParams(vmem_limit_bytes=24 * MIB),
        cost_estimate=pl.CostEstimate(flops=4_000_000, bytes_accessed=2_000_000, transcendentals=1000),
    )(peer, own, own_st)


def merge(msg_ref, out_ref):
    msg = msg_ref[...].astype(jnp.float32)
    st = msg[:, 48:56]
    rows = []
    for part in range(PARTS):
        at = part * 16
        top = column(st, part, 0)
        total = column(st, part, 1) + column(st, part, 2)
        dot = column(st, part, 3) + column(st, part, 4)
        factor = jnp.exp2((top - jnp.max(top, axis=0, keepdims=True)) * SCALE2)
        total = factor * total
        whole = jnp.sum(total, axis=0, keepdims=True)
        mean = jnp.sum(total * dot, axis=0, keepdims=True) / whole
        grad = jnp.sum(factor * msg[:, at : at + 8] + (factor * (dot - mean)) * msg[:, at + 8 : at + 16], axis=0)
        rows.append(grad * (SCALE / whole[0]))
    block = jnp.concatenate(rows, axis=0).astype(jnp.bfloat16)
    out_ref[...] = jnp.broadcast_to(block[None], out_ref.shape)


def merge_call(msg):
    return pl.pallas_call(
        merge,
        in_specs=[VMEM],
        out_specs=VMEM,
        out_shape=jax.ShapeDtypeStruct((32, 8 * PARTS, HD), jnp.bfloat16),
        compiler_params=pltpu.CompilerParams(vmem_limit_bytes=16 * MIB),
        cost_estimate=pl.CostEstimate(flops=4_000_000, bytes_accessed=800_000, transcendentals=1000),
    )(msg)


def squares_of(msg_ref, out_ref):
    grad = msg_ref[...].astype(jnp.float32)
    total = jnp.sum(jnp.sum(grad * grad, axis=0), axis=0, keepdims=True)
    out_ref[...] = jnp.broadcast_to(jnp.sum(total, axis=1, keepdims=True)[None], out_ref.shape)


def squares_call(msg):
    return pl.pallas_call(
        squares_of,
        in_specs=[VMEM],
        out_specs=VMEM,
        out_shape=jax.ShapeDtypeStruct((8, 8, HD), jnp.float32),
        compiler_params=pltpu.CompilerParams(vmem_limit_bytes=16 * MIB),
        cost_estimate=pl.CostEstimate(flops=200_000, bytes_accessed=230_000, transcendentals=0),
    )(msg)


def finish(own_ref, peer_ref, sum_ref, out_ref):
    core = lax.axis_index("c")
    squares = jnp.sum(sum_ref[...], axis=0)[:1]
    factor = 1.0 / jnp.sqrt(squares / (B * QT * HQ * HD) + EPSILON)
    for ref, odd in ((own_ref, core), (peer_ref, 1 - core)):
        rows = ref[...].astype(jnp.float32) * factor
        for part in range(PARTS):
            out_ref[2 * part + odd] = rows[:, part * 8 : part * 8 + 8].reshape(QT, 32, HD).astype(jnp.bfloat16)


def finish_call(own, peer, sums):
    return pl.pallas_call(
        finish,
        in_specs=[VMEM] * 3,
        out_specs=VMEM,
        out_shape=jax.ShapeDtypeStruct((B, QT, 32, HD), jnp.bfloat16),
        compiler_params=pltpu.CompilerParams(vmem_limit_bytes=16 * MIB),
        cost_estimate=pl.CostEstimate(flops=200_000, bytes_accessed=800_000, transcendentals=0),
    )(own, peer, sums)


def local(queries, key_cache, value_cache, grad_out, cache_len):
    swap = [(0, 1), (1, 0)]
    with jax.named_scope("attend"):
        peer, own, own_st = attend_call(cache_len, queries, key_cache, value_cache, grad_out)
    with jax.named_scope("pair"):
        peer = lax.ppermute(peer, "c", swap)
        msg = pair_up_call(peer, own, own_st)
    with jax.named_scope("exchange"):
        msg = lax.all_to_all(msg, ("z", "y"), 0, 0)
    with jax.named_scope("merge"):
        msg = merge_call(msg)
    with jax.named_scope("spread"):
        msg = lax.all_to_all(msg, ("z", "y"), 0, 0)
    with jax.named_scope("norm"):
        other = lax.ppermute(msg, "c", swap)
        sums = lax.all_to_all(squares_call(msg), ("c", "x"), 0, 0)
        return finish_call(msg, other, sums)


def solution(mesh):
    fine = Mesh(mesh.devices.reshape(8, 4, 2, 4), ("z", "y", "c", "x"))
    seq = ("z", "y", "c")
    placed = (
        P(None, None, "x", None),
        P(None, seq, "x", None),
        P(None, seq, "x", None),
        P(None, None, "x", None),
        P(),
    )
    return jax.shard_map(
        local, mesh=fine, in_specs=placed, out_specs=P(None, None, "x", None), check_vma=False
    )
```

time: 521 us -> 77.2 us (0.15); the launches traced: 511 us -> 77 us
  waiting for transfers between devices: 179 us -> 1.75 us
  blocking collectives: 166 us -> 48.3 us
  other arithmetic: 111 us -> 0 us
  matrix products: 35.6 us -> 0 us
  Pallas kernels: 0 us -> 18.2 us
  between operations: 14.2 us -> 0.03 us
  starting transfers between devices: 0.01 us -> 6.67 us
    psum x1 -> x0, waiting for transfers between devices: 179 us -> none  [local(): grad_sum = lax.psum(grad_part, 'seq')]
    all_gather x3 -> x0, blocking collectives: 157 us -> none  [joined(): gathered = jax.tree.map(lambda a: lax.all_gather(a, axis), part)]
    add x128 -> x0, other arithmetic: 106 us -> none  [the longest x63 53.2 us: combine_stats(): merged_total = left_total * left_factor + right_total * right_factor]
    all_to_all x0 -> x3, blocking collectives: none -> 48.3 us  [the longest x2 39.1 us: local(): msg = lax.all_to_all(msg, ('z', 'y'), 0, 0)]
    dot_general x3 -> x0, matrix products: 35.6 us -> none  [the longest x1 12.9 us: local(): jnp.einsum('btgih,bsgh->bgtis', grad_groups, value_cache, preferred_eleme...]
    pallas_call x0 -> x5, Pallas kernels: none -> 18.2 us  [the longest x1 15.4 us: attend_call(): pl.pallas_call(attend, in_specs=[pl.BlockSpec(memory_space=pltpu.SMEM), H...]
    psum x1 -> x0, blocking collectives: 9.01 us -> none  [local(): squares = lax.psum(jnp.sum(grad_sum * grad_sum), 'head')]
    ppermute x0 -> x2, starting transfers between devices: none -> 6.67 us  [the longest x1 3.52 us: local(): peer = lax.ppermute(peer, 'c', swap)]
  transfers between devices with their start and end apart: 1 -> 2, of which waited for: 1 -> 1; matrix products, arithmetic and copies ran while one was open for 0% -> 0% of each run, Pallas kernels for 0% -> 0%
where the time goes in v1:
time: 77.2 us; the launch traced here: 77 us
  blocking collectives  48.3 us (63%)
  Pallas kernels  18.2 us (24%)
  starting transfers between devices  6.67 us (9%)
  local copies, waits for them, and re-layouts  2.04 us (3%)
  waiting for transfers between devices  1.75 us (2%)
    all_to_all x2, blocking collectives, local(): msg = lax.all_to_all(msg, ('z', 'y'), 0, 0)  39.1 us
    pallas_call x1, Pallas kernels, attend_call(): pl.pallas_call(attend, in_specs=[pl.BlockSpec(memory_space=pltpu.SMEM), H...  15.4 us
    all_to_all x1, blocking collectives, local(): sums = lax.all_to_all(squares_call(msg), ('c', 'x'), 0, 0)  9.12 us
    ppermute x1, starting transfers between devices, local(): peer = lax.ppermute(peer, 'c', swap)  3.52 us
    ppermute x1, starting transfers between devices, local(): other = lax.ppermute(msg, 'c', swap)  3.15 us
    unnamed x4, local copies, waits for them, and re-layouts  2.04 us
    ppermute x1, waiting for transfers between devices, local(): peer = lax.ppermute(peer, 'c', swap)  1.75 us
  transfers between devices with their start and end apart: 2, of which 1 were waited for; matrix products, arithmetic and copies ran while one was open for 0% of the time, Pallas kernels for 0%

profile of v1, /device:TPU:1, one launch (start us, length us, event | category | flops | bytes accessed | tf_op | source)
XLA Modules:
  0.0 77.0 jit_solution(15141416172725685278)
XLA Ops:
  0.0 15.4 %attend.1 = (bf16[32,64,128]{2,1,0:T(8,128)(2,1)}, f32[32,48,128]{2,1,0:T(8,128)}, f32[32,8,128]{2,1,0:T(8,128)}) custom-call(s32[6]{0:T(128)} %len_ref.1, bf16[6,8,32,128]{3,2,1,0:T(8,128)(2,1)} %q_hbm.1, bf16[6,3840,128]{2,1,0:T(8,128)(2,1)} %bitcast.2, bf16[6,3840,128]{2,1,0:T(8,128)(2,1)} %bitcast.3, bf16[6,8,32,128]{3,2,1,0:T(8,128)(2,1)} %go_hbm.1), custom_call_target="tpu_custom_call" | custom-call | flops 4499999744 | bytes 14000000 | tf_op jit(solution)/shard_map/attend/pallas_call | solution.py:198
  15.4 3.5 %collective-permute-start = (bf16[32,64,128]{2,1,0:T(8,128)(2,1)}, bf16[32,64,128]{2,1,0:T(8,128)(2,1)S(1)}, u32[]{:S(2)}, u32[]{:S(2)}) collective-permute-start(bf16[32,64,128]{2,1,0:T(8,128)(2,1)} %get-tuple-element.8), channel_id=1, source_target_pairs={{0,4},{4,0},{1,5},{5,1},{2,6},{6,2},{3,7},{7,3},{8,12},{12,8},{9,1... | collective-permute-start | bytes 1572872 | tf_op jit(solution)/shard_map/pair/ppermute | solution.py:340
  18.9 1.7 %collective-permute-done.peer_ref = bf16[32,64,128]{2,1,0:T(8,128)(2,1)S(1)} collective-permute-done((bf16[32,64,128]{2,1,0:T(8,128)(2,1)}, bf16[32,64,128]{2,1,0:T(8,128)(2,1)S(1)}, u32[]{:S(2)}, u32[]{:S(2)}) %collective-permute-start) | collective-permute-done | bytes 524320 | tf_op jit(solution)/shard_map/pair/ppermute | solution.py:340
  20.7 0.0 copy-start
  20.7 1.1 %copy-done = f32[32,48,128]{2,1,0:T(8,128)S(1)} copy-done((f32[32,48,128]{2,1,0:T(8,128)S(1)}, f32[32,48,128]{2,1,0:T(8,128)}, u32[]{:S(2)}) %copy-start) | copy-done | bytes 786456
  21.8 0.0 copy-start.1
  21.8 0.9 %copy-done.1 = f32[32,8,128]{2,1,0:T(8,128)S(1)} copy-done((f32[32,8,128]{2,1,0:T(8,128)S(1)}, f32[32,8,128]{2,1,0:T(8,128)}, u32[]{:S(2)}) %copy-start.1) | copy-done | bytes 131096
  22.7 1.2 %pair.1 = bf16[32,56,128]{2,1,0:T(8,128)(2,1)S(1)} custom-call(bf16[32,64,128]{2,1,0:T(8,128)(2,1)S(1)} %collective-permute-done.peer_ref, f32[32,48,128]{2,1,0:T(8,128)S(1)} %copy-done, f32[32,8,128]{2,1,0:T(8,128)S(1)} %copy-done.1), custom_call_target="tpu_custom_call" | custom-call | flops 4000000 | bytes 2000000 | tf_op jit(solution)/shard_map/pair/pallas_call | solution.py:257
  24.0 24.7 %all_to_all.15.msg_ref = bf16[32,56,128]{2,1,0:T(8,128)(2,1)S(1)} all-to-all(bf16[32,56,128]{2,1,0:T(8,128)(2,1)S(1)} %pair.1), channel_id=1, replica_groups=mesh['z'=8,'y'=4,'c'=2,'x'=4] {'z','y'}, dimensions={0} | all-to-all | bytes 917504 | tf_op jit(solution)/shard_map/exchange/all_to_all | solution.py:343
  48.7 0.6 merge.1
  49.3 14.4 %all_to_all.16.msg_ref.own_ref = bf16[32,24,128]{2,1,0:T(8,128)(2,1)S(1)} all-to-all(bf16[32,24,128]{2,1,0:T(8,128)(2,1)S(1)} %merge.1), channel_id=1, replica_groups=mesh['z'=8,'y'=4,'c'=2,'x'=4] {'z','y'}, dimensions={0} | all-to-all | bytes 393216 | tf_op jit(solution)/shard_map/spread/all_to_all | solution.py:347
  63.7 3.2 %collective-permute-start.1 = (bf16[32,24,128]{2,1,0:T(8,128)(2,1)S(1)}, bf16[32,24,128]{2,1,0:T(8,128)(2,1)S(1)}, u32[]{:S(2)}, u32[]{:S(2)}) collective-permute-start(bf16[32,24,128]{2,1,0:T(8,128)(2,1)S(1)} %all_to_all.16.msg_ref.own_ref), channel_id=1, source_target_pairs={{0,4},{4,0},{1,5},{5,1},{2,6},{6,2},{3,7},{7,3},{8,12},{12,8},{9,1... | collective-permute-start | bytes 589832 | tf_op jit(solution)/shard_map/norm/ppermute | solution.py:349
  66.9 0.1 norm.2
  67.0 9.1 %all_to_all.17.sum_ref = f32[8,8,128]{2,1,0:T(8,128)S(1)} all-to-all(f32[8,8,128]{2,1,0:T(8,128)S(1)} %norm.2), channel_id=1, replica_groups=mesh['z'=8,'y'=4,'c'=2,'x'=4] {'c','x'}, dimensions={0} | all-to-all | bytes 65536 | tf_op jit(solution)/shard_map/norm/all_to_all | solution.py:350
  76.1 0.0 collective-permute-done.1.peer_ref
  76.1 0.8 %norm.3 = bf16[6,8,32,128]{3,2,1,0:T(8,128)(2,1)} custom-call(bf16[32,24,128]{2,1,0:T(8,128)(2,1)S(1)} %all_to_all.16.msg_ref.own_ref, bf16[32,24,128]{2,1,0:T(8,128)(2,1)S(1)} %collective-permute-done.1.peer_ref, f32[8,8,128]{2,1,0:T(8,128)S(1)} %all_to_all.17.sum_ref), custom_call_target="tpu_custom_call" | custom-call | flops 200000 | bytes 800000 | tf_op jit(solution)/shard_map/norm/pallas_call | solution.py:325
Async XLA Ops:
  15.4 5.3 %collective-permute-start = (bf16[32,64,128]{2,1,0:T(8,128)(2,1)}, bf16[32,64,128]{2,1,0:T(8,128)(2,1)S(1)}, u32[]{:S(2)}, u32[]{:S(2)}) collective-permute-start(bf16[32,64,128]{2,1,0:T(8,128)(2,1)} %get-tuple-element.8), channel_id=1, source_target_pairs={{0,4},{4,0},{1,5},{5,1},{2,6},{6,2},{3,7},{7,3},{8,12},{12,8},{9,1... | collective-permute-start | bytes 1572872 | tf_op jit(solution)/shard_map/pair/ppermute | solution.py:340
  20.7 1.1 %copy-start = (f32[32,48,128]{2,1,0:T(8,128)S(1)}, f32[32,48,128]{2,1,0:T(8,128)}, u32[]{:S(2)}) copy-start(f32[32,48,128]{2,1,0:T(8,128)} %get-tuple-element.9.own_ref) | copy-start | bytes 2359300
  21.8 0.9 %copy-start.1 = (f32[32,8,128]{2,1,0:T(8,128)S(1)}, f32[32,8,128]{2,1,0:T(8,128)}, u32[]{:S(2)}) copy-start(f32[32,8,128]{2,1,0:T(8,128)} %get-tuple-element.10.own_st_ref) | copy-start | bytes 393220
  63.7 12.4 %collective-permute-start.1 = (bf16[32,24,128]{2,1,0:T(8,128)(2,1)S(1)}, bf16[32,24,128]{2,1,0:T(8,128)(2,1)S(1)}, u32[]{:S(2)}, u32[]{:S(2)}) collective-permute-start(bf16[32,24,128]{2,1,0:T(8,128)(2,1)S(1)} %all_to_all.16.msg_ref.own_ref), channel_id=1, source_target_pairs={{0,4},{4,0},{1,5},{5,1},{2,6},{6,2},{3,7},{7,3},{8,12},{12,8},{9,1... | collective-permute-start | bytes 589832 | tf_op jit(solution)/shard_map/norm/ppermute | solution.py:349

commit v2 on v1

--- a/solution.py
+++ b/solution.py
@@ -19,7 +19,6 @@
 SCALE = 1.0 / math.sqrt(HD)
 SCALE2 = SCALE * math.log2(math.e)
 CHUNK = 256
-TILES = CHUNK // 8
 PARTS = 3
 SLOT = 56
 MIB = 1024 * 1024
@@ -34,97 +33,105 @@
 
 def attend(
     len_ref, q_hbm, k_hbm, v_hbm, go_hbm, peer_ref, own_ref, own_st_ref,
-    q_buf, go_buf, k_buf, v_buf, s_a, s_b, s_c, g_a, g_b, g_c, sems,
+    q_buf, go_buf, k_buf, v_buf, s_a, s_b, s_c, g_a, g_b, g_c,
+    d_a, d_b, d_c, f_a, f_b, f_c, f_d, sems,
 ):
     core = lax.axis_index("c")
     count, rows = k_buf.shape[0], k_buf.shape[1]
     span = rows // 2
-    chunks = rows // CHUNK
+    chunks = -(-span // CHUNK)
+    flat = (f_a, f_b, f_c, f_d)
     start = ((lax.axis_index("z") * 4 + lax.axis_index("y")) * 2 + core) * span
 
     def sequence(j):
         return 2 * j + 1 - core if j < PARTS else 2 * (j - PARTS) + core
 
-    small = [
-        pltpu.make_async_copy(q_hbm, q_buf, sems.at[2 * count]),
-        pltpu.make_async_copy(go_hbm, go_buf, sems.at[2 * count + 1]),
-    ]
-    keys = [pltpu.make_async_copy(k_hbm.at[sequence(j)], k_buf.at[j], sems.at[2 * j]) for j in range(count)]
-    values = [pltpu.make_async_copy(v_hbm.at[sequence(j)], v_buf.at[j], sems.at[2 * j + 1]) for j in range(count)]
-    small[0].start()
-    keys[0].start()
-    small[1].start()
-    values[0].start()
-    for j in range(1, count):
-        keys[j].start()
-        values[j].start()
-
-    scores, probs = (s_a, s_b, s_c), (g_a, g_b, g_c)
-    even8 = lax.broadcasted_iota(jnp.int32, (8, 128), 0) % 2 == 0
-    odd_row = lax.broadcasted_iota(jnp.int32, (CHUNK, 128), 0) % 2 == 1
-    keep_odd = odd_row.astype(jnp.float32).astype(jnp.bfloat16)
-    keep_even = (1.0 - odd_row.astype(jnp.float32)).astype(jnp.bfloat16)
-    lead = lax.broadcasted_iota(jnp.int32, (8, 128), 1) // 16 - lax.broadcasted_iota(jnp.int32, (8, 128), 0) // 2
-    tile_start = lax.broadcasted_iota(jnp.int32, (TILES, 8, 128), 0) * 4
+    def place(i):
+        first = i * CHUNK
+        return first, min(CHUNK, span - first)
+
+    def whole(source, target, base):
+        return [
+            pltpu.make_async_copy(source.at[sequence(j)], target.at[j], sems.at[base + j]) for j in range(count)
+        ]
+
+    keys, values = whole(k_hbm, k_buf, 0), whole(v_hbm, v_buf, count)
+    small = list(zip(whole(q_hbm, q_buf, 2 * count), whole(go_hbm, go_buf, 3 * count)))
+    for j in range(count):
+        for copy in (small[j][0], keys[j], small[j][1], values[j]):
+            copy.start()
+
+    scores, probs, splits = (s_a, s_b, s_c), (g_a, g_b, g_c), (d_a, d_b, d_c)
+    lead = lax.broadcasted_iota(jnp.int32, (8, 256), 1) % 128 // 16 - lax.broadcasted_iota(jnp.int32, (8, 256), 0)
 
     def turned(x):
-        both = jnp.concatenate([x[:, :16].reshape(128, HD), x[:, 16:].reshape(128, HD)], axis=0)
-        return both.T
-
-    def sides(x, reduce, fill):
-        return (
-            reduce(jnp.where(even8, x, fill), axis=0, keepdims=True),
-            reduce(jnp.where(even8, fill, x), axis=0, keepdims=True),
+        blank = jnp.zeros((HD, 128), jnp.bfloat16)
+        left = jnp.concatenate([x[:, :16].reshape(128, HD).T, blank], axis=0)
+        right = jnp.concatenate([blank, x[:, 16:].reshape(128, HD).T], axis=0)
+        return jnp.concatenate([left, right], axis=1)
+
+    def sides(x, reduce):
+        return reduce(x, axis=0, keepdims=True)
+
+    def split(source, j, i, which):
+        first, size = place(i)
+        scr = flat[which * 2 + i % 2]
+        scr[: 2 * size, :] = source[j, 2 * first : 2 * (first + size), :].astype(jnp.float32)
+        return jnp.concatenate(
+            [scr[pl.ds(side, size, stride=2), :].astype(jnp.bfloat16) for side in range(2)], axis=1
         )
 
     def score_step(j, i, qt, gt, room, top):
-        at = slice(i * CHUNK, (i + 1) * CHUNK)
-        s = jnp.dot(k_buf[j, at, :], qt, preferred_element_type=jnp.float32)
-        s = jnp.where(odd_row, s[:, 128:], s[:, :128]).reshape(TILES, 8, 128)
-        s = jnp.where((room + lead - i * (CHUNK // 2))[None] >= tile_start, s, NEGATIVE)
-        scores[j % 3][at, :] = s.reshape(CHUNK, 128)
-        g = jnp.dot(v_buf[j, at, :], gt, preferred_element_type=jnp.float32)
-        probs[j % 3][at, :] = jnp.where(odd_row, g[:, 128:], g[:, :128])
+        first, size = place(i)
+        at = slice(first, first + size)
+        kd = split(k_buf, j, i, 0)
+        splits[j % 3][at, :] = kd
+        s = jnp.dot(kd, qt, preferred_element_type=jnp.float32).reshape(size // 8, 8, 256)
+        tile_start = lax.broadcasted_iota(jnp.int32, (size // 8, 8, 256), 0) * 8
+        s = jnp.where((room + lead - first)[None] >= tile_start, s, NEGATIVE)
+        scores[j % 3][at, :] = s.reshape(size, 256)
+        vd = split(v_buf, j, i, 1)
+        probs[j % 3][at, :] = jnp.dot(vd, gt, preferred_element_type=jnp.float32)
         return jnp.maximum(top, jnp.max(s, axis=0))
 
     def weight_step(j, i, tops, total, dot):
-        at = slice(i * CHUNK, (i + 1) * CHUNK)
-        s = scores[j % 3][at, :].reshape(TILES, 8, 128)
+        first, size = place(i)
+        at = slice(first, first + size)
+        s = scores[j % 3][at, :].reshape(size // 8, 8, 256)
         w = jnp.exp2((s - tops[None]) * SCALE2)
-        scores[j % 3][at, :] = w.reshape(CHUNK, 128)
-        wg = w * probs[j % 3][at, :].reshape(TILES, 8, 128)
+        scores[j % 3][at, :] = w.reshape(size, 256)
+        wg = w * probs[j % 3][at, :].reshape(size // 8, 8, 256)
         return total + jnp.sum(w, axis=0), dot + jnp.sum(wg, axis=0)
 
     def term_step(j, i, dots, acc):
-        at = slice(i * CHUNK, (i + 1) * CHUNK)
-        w = scores[j % 3][at, :].reshape(TILES, 8, 128)
-        p = w * (probs[j % 3][at, :].reshape(TILES, 8, 128) - dots[None])
-        pw = jnp.concatenate([p.reshape(CHUNK, 128), w.reshape(CHUNK, 128)], axis=1).astype(jnp.bfloat16)
-        kc = k_buf[j, at, :]
-        kk = jnp.concatenate([kc * keep_even, kc * keep_odd], axis=1)
-        return acc + lax.dot_general(pw, kk, FIRST, preferred_element_type=jnp.float32)
+        first, size = place(i)
+        at = slice(first, first + size)
+        w = scores[j % 3][at, :]
+        p = w * (probs[j % 3][at, :] - dots)
+        out = []
+        for side in range(2):
+            cols = slice(side * 128, side * 128 + 128)
+            pw = jnp.concatenate([p[:, cols], w[:, cols]], axis=1).astype(jnp.bfloat16)
+            out.append(
+                acc[side]
+                + lax.dot_general(splits[j % 3][at, cols], pw, FIRST, preferred_element_type=jnp.float32)
+            )
+        return out
 
     def prepare(j):
         seq = sequence(j)
-        keys[j].wait()
-        values[j].wait()
-        return turned(q_buf[seq]), turned(go_buf[seq]), len_ref[seq] - QT - start
-
-    def reference_of(top):
-        return [high(jnp.maximum(m, FLOOR)) for m in sides(top, jnp.max, NEGATIVE)]
+        for copy in (*small[j], keys[j], values[j]):
+            copy.wait()
+        return turned(q_buf[j]), turned(go_buf[j]), len_ref[seq] - QT - start
 
     def means_of(total, dot):
-        totals = sides(total, jnp.sum, 0.0)
-        dots = [
-            jnp.where(t > 0.0, d / jnp.where(t > 0.0, t, 1.0), 0.0)
-            for t, d in zip(totals, sides(dot, jnp.sum, 0.0))
-        ]
-        return totals, dots
+        total, dot = sides(total, jnp.sum), sides(dot, jnp.sum)
+        return total, jnp.where(total > 0.0, dot / jnp.where(total > 0.0, total, 1.0), 0.0)
 
     def store(j, acc, tops, totals, dots):
         pieces = []
-        for half in (acc[:128], acc[128:]):
-            pair = [half[:, side * 128 : (side + 1) * 128].reshape(8, 16, 128) for side in range(2)]
+        for half in (slice(0, 128), slice(128, 256)):
+            pair = [acc[side][:, half].T.reshape(8, 16, 128) for side in range(2)]
             pieces.append(jnp.concatenate(pair, axis=1).reshape(32, 8, 128))
         both = jnp.concatenate(pieces, axis=1)
         part = j % PARTS
@@ -134,40 +141,34 @@
             own_ref[:, part * 16 : part * 16 + 16, :] = both
         sub = lax.broadcasted_iota(jnp.int32, (8, 128), 0)
         for side in range(2):
-            if j < PARTS:
-                t, d = totals[side], dots[side]
-                cols = (tops[side], high(t), t - high(t), high(d), d - high(d))
-            else:
-                cols = (tops[side], totals[side], dots[side])
+            at = slice(side * 128, side * 128 + 128)
+            m, t, d = tops[:, at], totals[:, at], dots[:, at]
+            cols = (m, high(t), t - high(t), high(d), d - high(d)) if j < PARTS else (m, t, d)
             block = jnp.zeros((8, 128), jnp.float32)
             for k, col in enumerate(cols):
                 block = jnp.where(sub == k, col, block)
             blocks[j // PARTS, side, part] = block
 
     blocks = {}
-    for copy in small:
-        copy.wait()
-    zero8 = jnp.zeros((8, 128), jnp.float32)
+    zero8 = jnp.zeros((8, 256), jnp.float32)
     stats = {}
     for n in range(count + 2):
         first, second, third = n, n - 1, n - 2
         if first < count:
             ready = prepare(first)
-            top = jnp.full((8, 128), NEGATIVE, jnp.float32)
+            top = jnp.full((8, 256), NEGATIVE, jnp.float32)
         if 0 <= second < count:
-            tops = reference_of(last_top)
-            tops8 = jnp.where(even8, *tops)
+            tops = high(jnp.maximum(sides(last_top, jnp.max), FLOOR))
             total, dot = zero8, zero8
         if 0 <= third:
-            dots8 = jnp.where(even8, *stats[third][2])
-            acc = jnp.zeros((256, 256), jnp.float32)
+            acc = [jnp.zeros((128, 256), jnp.float32)] * 2
         for i in range(chunks):
             if 0 <= third:
-                acc = term_step(third, i, dots8, acc)
+                acc = term_step(third, i, stats[third][2], acc)
             if first < count:
                 top = score_step(first, i, *ready, top)
             if 0 <= second < count:
-                total, dot = weight_step(second, i, tops8, total, dot)
+                total, dot = weight_step(second, i, tops, total, dot)
         if 0 <= third:
             store(third, acc, *stats[third])
         if 0 <= second < count:
@@ -192,27 +193,31 @@
 
 def attend_call(lengths, q, k, v, go):
     count, span = k.shape[0], k.shape[1]
-    k = k.reshape(count, span * 2, HD)
-    v = v.reshape(count, span * 2, HD)
-    wide = pltpu.VMEM((span * 2, 128), jnp.float32)
+    q, k, v, go = (
+        pltpu.with_memory_space_constraint(x, pltpu.HBM)
+        for x in (q, k.reshape(count, span * 2, HD), v.reshape(count, span * 2, HD), go)
+    )
+    wide = pltpu.VMEM((span, 256), jnp.float32)
+    slim = pltpu.VMEM((span, 256), jnp.bfloat16)
+    flat = pltpu.VMEM((2 * CHUNK, HD), jnp.float32)
     return pl.pallas_call(
         attend,
         in_specs=[pl.BlockSpec(memory_space=pltpu.SMEM), HBM, HBM, HBM, HBM],
         out_specs=[VMEM, VMEM, VMEM],
         out_shape=[
-            jax.ShapeDtypeStruct((32, 64, HD), jnp.bfloat16),
-            jax.ShapeDtypeStruct((32, 48, HD), jnp.float32),
-            jax.ShapeDtypeStruct((32, 8, HD), jnp.float32),
+            pltpu.VMEM((32, 64, HD), jnp.bfloat16),
+            pltpu.VMEM((32, 48, HD), jnp.float32),
+            pltpu.VMEM((32, 8, HD), jnp.float32),
         ],
         scratch_shapes=[
             pltpu.VMEM(q.shape, jnp.bfloat16),
             pltpu.VMEM(go.shape, jnp.bfloat16),
             pltpu.VMEM(k.shape, jnp.bfloat16),
             pltpu.VMEM(v.shape, jnp.bfloat16),
-            wide, wide, wide, wide, wide, wide,
-            pltpu.SemaphoreType.DMA((2 * count + 2,)),
+            wide, wide, wide, wide, wide, wide, slim, slim, slim, flat, flat, flat, flat,
+            pltpu.SemaphoreType.DMA((4 * count,)),
         ],
-        compiler_params=pltpu.CompilerParams(vmem_limit_bytes=60 * MIB),
+        compiler_params=pltpu.CompilerParams(vmem_limit_bytes=56 * MIB),
         cost_estimate=pl.CostEstimate(flops=4_500_000_000, bytes_accessed=14_000_000, transcendentals=3_000_000),
     )(lengths, q, k, v, go)
 

time: 77.2 us -> 71.6 us (0.927)
  Pallas kernels: 18.2 us -> 15 us
  local copies, waits for them, and re-layouts: 2.04 us -> 0 us
    pallas_call x1, Pallas kernels: 15.4 us -> 12.2 us  [attend_call(): pl.pallas_call(attend, in_specs=[pl.BlockSpec(memory_space=pltpu.SMEM), H...]
    unnamed x4 -> x0, local copies, waits for them, and re-layouts: 2.04 us -> none
where the time goes in v2:
time: 71.6 us; the launch traced here: 71.4 us
  blocking collectives  48.3 us (67%)
  Pallas kernels  15 us (21%)
  starting transfers between devices  6.49 us (9%)
  waiting for transfers between devices  1.54 us (2%)
    all_to_all x2, blocking collectives, local(): msg = lax.all_to_all(msg, ('z', 'y'), 0, 0)  39.1 us
    pallas_call x1, Pallas kernels, attend_call(): pl.pallas_call(attend, in_specs=[pl.BlockSpec(memory_space=pltpu.SMEM), H...  12.2 us
    all_to_all x1, blocking collectives, local(): sums = lax.all_to_all(squares_call(msg), ('c', 'x'), 0, 0)  9.13 us
    ppermute x1, starting transfers between devices, local(): peer = lax.ppermute(peer, 'c', swap)  3.34 us
    ppermute x1, starting transfers between devices, local(): other = lax.ppermute(msg, 'c', swap)  3.15 us
    ppermute x1, waiting for transfers between devices, local(): peer = lax.ppermute(peer, 'c', swap)  1.54 us
  transfers between devices with their start and end apart: 2, of which 1 were waited for; matrix products, arithmetic and copies ran while one was open for 0% of the time, Pallas kernels for 0%

profile of v2, /device:TPU:1, one launch (start us, length us, event | category | flops | bytes accessed | tf_op | source)
XLA Modules:
  0.0 71.4 jit_solution(341450482599172113)
XLA Ops:
  0.0 12.2 %attend.1 = (bf16[32,64,128]{2,1,0:T(8,128)(2,1)S(1)}, f32[32,48,128]{2,1,0:T(8,128)S(1)}, f32[32,8,128]{2,1,0:T(8,128)S(1)}) custom-call(s32[6]{0:T(128)} %len_ref.1, bf16[6,8,32,128]{3,2,1,0:T(8,128)(2,1)} %q_hbm.1, bf16[6,3840,128]{2,1,0:T(8,128)(2,1)} %bitcast.2, bf16[6,3840,128]{2,1,0:T(8,128)(2,1)} %bitcast.3, bf16[6,8,32,128]{3,2,1,0:T(8,128)(2,1)} %go_hbm.1), custom_call_target="tpu_custom_call" | custom-call | flops 4499999744 | bytes 14000000 | tf_op jit(solution)/shard_map/attend/pallas_call | solution.py:203
  12.2 3.3 %collective-permute-start = (bf16[32,64,128]{2,1,0:T(8,128)(2,1)S(1)}, bf16[32,64,128]{2,1,0:T(8,128)(2,1)S(1)}, u32[]{:S(2)}, u32[]{:S(2)}) collective-permute-start(bf16[32,64,128]{2,1,0:T(8,128)(2,1)S(1)} %get-tuple-element.8), channel_id=1, source_target_pairs={{0,4},{4,0},{1,5},{5,1},{2,6},{6,2},{3,7},{7,3},{8,12},{12,8},{9,1... | collective-permute-start | bytes 1572872 | tf_op jit(solution)/shard_map/pair/ppermute | solution.py:345
  15.6 1.5 %collective-permute-done.peer_ref = bf16[32,64,128]{2,1,0:T(8,128)(2,1)S(1)} collective-permute-done((bf16[32,64,128]{2,1,0:T(8,128)(2,1)S(1)}, bf16[32,64,128]{2,1,0:T(8,128)(2,1)S(1)}, u32[]{:S(2)}, u32[]{:S(2)}) %collective-permute-start) | collective-permute-done | bytes 524320 | tf_op jit(solution)/shard_map/pair/ppermute | solution.py:345
  17.1 1.2 %pair.1 = bf16[32,56,128]{2,1,0:T(8,128)(2,1)S(1)} custom-call(bf16[32,64,128]{2,1,0:T(8,128)(2,1)S(1)} %collective-permute-done.peer_ref, f32[32,48,128]{2,1,0:T(8,128)S(1)} %get-tuple-element.9.own_ref, f32[32,8,128]{2,1,0:T(8,128)S(1)} %get-tuple-element.10.own_st_ref), custom_call_target="tpu_custom_call" | custom-call | flops 4000000 | bytes 2000000 | tf_op jit(solution)/shard_map/pair/pallas_call | solution.py:262
  18.4 24.7 %all_to_all.15.msg_ref = bf16[32,56,128]{2,1,0:T(8,128)(2,1)S(1)} all-to-all(bf16[32,56,128]{2,1,0:T(8,128)(2,1)S(1)} %pair.1), channel_id=1, replica_groups=mesh['z'=8,'y'=4,'c'=2,'x'=4] {'z','y'}, dimensions={0} | all-to-all | bytes 917504 | tf_op jit(solution)/shard_map/exchange/all_to_all | solution.py:348
  43.1 0.6 merge.1
  43.7 14.4 %all_to_all.16.msg_ref.own_ref = bf16[32,24,128]{2,1,0:T(8,128)(2,1)S(1)} all-to-all(bf16[32,24,128]{2,1,0:T(8,128)(2,1)S(1)} %merge.1), channel_id=1, replica_groups=mesh['z'=8,'y'=4,'c'=2,'x'=4] {'z','y'}, dimensions={0} | all-to-all | bytes 393216 | tf_op jit(solution)/shard_map/spread/all_to_all | solution.py:352
  58.1 3.2 %collective-permute-start.1 = (bf16[32,24,128]{2,1,0:T(8,128)(2,1)S(1)}, bf16[32,24,128]{2,1,0:T(8,128)(2,1)S(1)}, u32[]{:S(2)}, u32[]{:S(2)}) collective-permute-start(bf16[32,24,128]{2,1,0:T(8,128)(2,1)S(1)} %all_to_all.16.msg_ref.own_ref), channel_id=1, source_target_pairs={{0,4},{4,0},{1,5},{5,1},{2,6},{6,2},{3,7},{7,3},{8,12},{12,8},{9,1... | collective-permute-start | bytes 589832 | tf_op jit(solution)/shard_map/norm/ppermute | solution.py:354
  61.3 0.1 norm.2
  61.4 9.1 %all_to_all.17.sum_ref = f32[8,8,128]{2,1,0:T(8,128)S(1)} all-to-all(f32[8,8,128]{2,1,0:T(8,128)S(1)} %norm.2), channel_id=1, replica_groups=mesh['z'=8,'y'=4,'c'=2,'x'=4] {'c','x'}, dimensions={0} | all-to-all | bytes 65536 | tf_op jit(solution)/shard_map/norm/all_to_all | solution.py:355
  70.5 0.0 collective-permute-done.1.peer_ref
  70.5 0.8 %norm.3 = bf16[6,8,32,128]{3,2,1,0:T(8,128)(2,1)} custom-call(bf16[32,24,128]{2,1,0:T(8,128)(2,1)S(1)} %all_to_all.16.msg_ref.own_ref, bf16[32,24,128]{2,1,0:T(8,128)(2,1)S(1)} %collective-permute-done.1.peer_ref, f32[8,8,128]{2,1,0:T(8,128)S(1)} %all_to_all.17.sum_ref), custom_call_target="tpu_custom_call" | custom-call | flops 200000 | bytes 800000 | tf_op jit(solution)/shard_map/norm/pallas_call | solution.py:330
Async XLA Ops:
  12.2 4.9 %collective-permute-start = (bf16[32,64,128]{2,1,0:T(8,128)(2,1)S(1)}, bf16[32,64,128]{2,1,0:T(8,128)(2,1)S(1)}, u32[]{:S(2)}, u32[]{:S(2)}) collective-permute-start(bf16[32,64,128]{2,1,0:T(8,128)(2,1)S(1)} %get-tuple-element.8), channel_id=1, source_target_pairs={{0,4},{4,0},{1,5},{5,1},{2,6},{6,2},{3,7},{7,3},{8,12},{12,8},{9,1... | collective-permute-start | bytes 1572872 | tf_op jit(solution)/shard_map/pair/ppermute | solution.py:345
  58.1 12.4 %collective-permute-start.1 = (bf16[32,24,128]{2,1,0:T(8,128)(2,1)S(1)}, bf16[32,24,128]{2,1,0:T(8,128)(2,1)S(1)}, u32[]{:S(2)}, u32[]{:S(2)}) collective-permute-start(bf16[32,24,128]{2,1,0:T(8,128)(2,1)S(1)} %all_to_all.16.msg_ref.own_ref), channel_id=1, source_target_pairs={{0,4},{4,0},{1,5},{5,1},{2,6},{6,2},{3,7},{7,3},{8,12},{12,8},{9,1... | collective-permute-start | bytes 589832 | tf_op jit(solution)/shard_map/norm/ppermute | solution.py:354

commit v3 on v2

--- a/solution.py
+++ b/solution.py
@@ -62,7 +62,7 @@
             copy.start()
 
     scores, probs, splits = (s_a, s_b, s_c), (g_a, g_b, g_c), (d_a, d_b, d_c)
-    lead = lax.broadcasted_iota(jnp.int32, (8, 256), 1) % 128 // 16 - lax.broadcasted_iota(jnp.int32, (8, 256), 0)
+    lead = lax.broadcasted_iota(jnp.int32, (8, 128), 1) // 16 - lax.broadcasted_iota(jnp.int32, (8, 128), 0)
 
     def turned(x):
         blank = jnp.zeros((HD, 128), jnp.bfloat16)
@@ -86,13 +86,18 @@
         at = slice(first, first + size)
         kd = split(k_buf, j, i, 0)
         splits[j % 3][at, :] = kd
-        s = jnp.dot(kd, qt, preferred_element_type=jnp.float32).reshape(size // 8, 8, 256)
-        tile_start = lax.broadcasted_iota(jnp.int32, (size // 8, 8, 256), 0) * 8
-        s = jnp.where((room + lead - first)[None] >= tile_start, s, NEGATIVE)
-        scores[j % 3][at, :] = s.reshape(size, 256)
+        s = jnp.dot(kd, qt, preferred_element_type=jnp.float32)
+        tile_start = lax.broadcasted_iota(jnp.int32, (size // 8, 8, 128), 0) * 8
+        visible = (room + lead - first)[None] >= tile_start
+        peaks = []
+        for side in range(2):
+            cols = slice(side * 128, side * 128 + 128)
+            half = jnp.where(visible, s[:, cols].reshape(size // 8, 8, 128), NEGATIVE)
+            scores[j % 3][at, cols] = half.reshape(size, 128)
+            peaks.append(jnp.max(half, axis=0))
         vd = split(v_buf, j, i, 1)
         probs[j % 3][at, :] = jnp.dot(vd, gt, preferred_element_type=jnp.float32)
-        return jnp.maximum(top, jnp.max(s, axis=0))
+        return jnp.maximum(top, jnp.concatenate(peaks, axis=1))
 
     def weight_step(j, i, tops, total, dot):
         first, size = place(i)
@@ -222,39 +227,45 @@
     )(lengths, q, k, v, go)
 
 
-def column(st, part, k):
-    at = 8 * part + k
-    return st[:, :, at : at + 1]
+def shifted(st, k):
+    return pltpu.roll(st.reshape(256, 128), 128 - k, 1).reshape(32, 8, 128)
+
+
+def spread_stats(st):
+    return st, shifted(st, 1) + shifted(st, 2), shifted(st, 3) + shifted(st, 4)
+
+
+def column(x, part):
+    return x[..., 8 * part : 8 * part + 1]
 
 
 def pair_up(peer_ref, own_ref, own_st_ref, out_ref):
     peer = peer_ref[...].astype(jnp.float32)
     own = own_ref[...]
-    peer_st, own_st = peer[:, 48:56], own_st_ref[...]
-    lane = lax.broadcasted_iota(jnp.int32, (32, 8, 128), 2)
-    st = jnp.zeros((32, 8, 128), jnp.float32)
+    own_st = own_st_ref[...]
+    top_a, total_a, dot_a = own_st, shifted(own_st, 1), shifted(own_st, 2)
+    top_b, total_b, dot_b = spread_stats(peer[:, 48:56])
+    top = jnp.maximum(top_a, top_b)
+    factor_a = jnp.exp2((top_a - top) * SCALE2)
+    factor_b = jnp.exp2((top_b - top) * SCALE2)
+    total_a, total_b = factor_a * total_a, factor_b * total_b
+    total = total_a + total_b
+    dot = (total_a * dot_a + total_b * dot_b) / jnp.where(total > 0.0, total, 1.0)
+    lag_a, lag_b = factor_a * (dot_a - dot), factor_b * (dot_b - dot)
     pieces = []
     for part in range(PARTS):
         at = part * 16
-        top_a, total_a, dot_a = (column(own_st, part, k) for k in range(3))
-        top_b = column(peer_st, part, 0)
-        total_b = column(peer_st, part, 1) + column(peer_st, part, 2)
-        dot_b = column(peer_st, part, 3) + column(peer_st, part, 4)
-        top = jnp.maximum(top_a, top_b)
-        factor_a = jnp.exp2((top_a - top) * SCALE2)
-        factor_b = jnp.exp2((top_b - top) * SCALE2)
-        total_a, total_b = factor_a * total_a, factor_b * total_b
-        total = total_a + total_b
-        dot = (total_a * dot_a + total_b * dot_b) / jnp.where(total > 0.0, total, 1.0)
         term_a, term_b = own[:, at : at + 8], peer[:, at : at + 8]
         mass_a, mass_b = own[:, at + 8 : at + 16], peer[:, at + 8 : at + 16]
+        take_a, take_b = column(factor_a, part), column(factor_b, part)
         pieces.append(
-            factor_a * term_a + (factor_a * (dot_a - dot)) * mass_a
-            + (factor_b * term_b + (factor_b * (dot_b - dot)) * mass_b)
+            take_a * term_a + column(lag_a, part) * mass_a + (take_b * term_b + column(lag_b, part) * mass_b)
         )
-        pieces.append(factor_a * mass_a + factor_b * mass_b)
-        for k, col in enumerate((top, high(total), total - high(total), high(dot), dot - high(dot))):
-            st = jnp.where(lane == 8 * part + k, col, st)
+        pieces.append(take_a * mass_a + take_b * mass_b)
+    lane = lax.broadcasted_iota(jnp.int32, (32, 8, 128), 2)
+    st = jnp.zeros((32, 8, 128), jnp.float32)
+    for k, value in enumerate((top, high(total), total - high(total), high(dot), dot - high(dot))):
+        st = jnp.where((lane % 8 == k) & (lane < 8 * PARTS), shifted(value, 128 - k) if k else value, st)
     out_ref[...] = jnp.concatenate(pieces + [st], axis=1).astype(jnp.bfloat16)
 
 
@@ -271,19 +282,19 @@
 
 def merge(msg_ref, out_ref):
     msg = msg_ref[...].astype(jnp.float32)
-    st = msg[:, 48:56]
+    top, total, dot = spread_stats(msg[:, 48:56])
+    factor = jnp.exp2((top - jnp.max(top, axis=0, keepdims=True)) * SCALE2)
+    total = factor * total
+    whole = jnp.sum(total, axis=0, keepdims=True)
+    lag = factor * (dot - jnp.sum(total * dot, axis=0, keepdims=True) / whole)
+    scale = (SCALE / whole)[0]
     rows = []
     for part in range(PARTS):
         at = part * 16
-        top = column(st, part, 0)
-        total = column(st, part, 1) + column(st, part, 2)
-        dot = column(st, part, 3) + column(st, part, 4)
-        factor = jnp.exp2((top - jnp.max(top, axis=0, keepdims=True)) * SCALE2)
-        total = factor * total
-        whole = jnp.sum(total, axis=0, keepdims=True)
-        mean = jnp.sum(total * dot, axis=0, keepdims=True) / whole
-        grad = jnp.sum(factor * msg[:, at : at + 8] + (factor * (dot - mean)) * msg[:, at + 8 : at + 16], axis=0)
-        rows.append(grad * (SCALE / whole[0]))
+        grad = jnp.sum(
+            column(factor, part) * msg[:, at : at + 8] + column(lag, part) * msg[:, at + 8 : at + 16], axis=0
+        )
+        rows.append(grad * column(scale, part))
     block = jnp.concatenate(rows, axis=0).astype(jnp.bfloat16)
     out_ref[...] = jnp.broadcast_to(block[None], out_ref.shape)
 

time: 71.6 us -> 70.7 us (0.987)
  Pallas kernels: 15 us -> 14.2 us
where the time goes in v3:
time: 70.7 us; the launch traced here: 70.5 us
  blocking collectives  48.3 us (68%)
  Pallas kernels  14.2 us (20%)
  starting transfers between devices  6.49 us (9%)
  waiting for transfers between devices  1.54 us (2%)
    all_to_all x2, blocking collectives, local(): msg = lax.all_to_all(msg, ('z', 'y'), 0, 0)  39.1 us
    pallas_call x1, Pallas kernels, attend_call(): pl.pallas_call(attend, in_specs=[pl.BlockSpec(memory_space=pltpu.SMEM), H...  12.1 us
    all_to_all x1, blocking collectives, local(): sums = lax.all_to_all(squares_call(msg), ('c', 'x'), 0, 0)  9.11 us
    ppermute x1, starting transfers between devices, local(): peer = lax.ppermute(peer, 'c', swap)  3.34 us
    ppermute x1, starting transfers between devices, local(): other = lax.ppermute(msg, 'c', swap)  3.15 us
    ppermute x1, waiting for transfers between devices, local(): peer = lax.ppermute(peer, 'c', swap)  1.54 us
  transfers between devices with their start and end apart: 2, of which 1 were waited for; matrix products, arithmetic and copies ran while one was open for 0% of the time, Pallas kernels for 0%

profile of v3, /device:TPU:1, one launch (start us, length us, event | category | flops | bytes accessed | tf_op | source)
XLA Modules:
  0.0 70.5 jit_solution(626989196397262455)
XLA Ops:
  0.0 12.1 %attend.1 = (bf16[32,64,128]{2,1,0:T(8,128)(2,1)S(1)}, f32[32,48,128]{2,1,0:T(8,128)S(1)}, f32[32,8,128]{2,1,0:T(8,128)S(1)}) custom-call(s32[6]{0:T(128)} %len_ref.1, bf16[6,8,32,128]{3,2,1,0:T(8,128)(2,1)} %q_hbm.1, bf16[6,3840,128]{2,1,0:T(8,128)(2,1)} %bitcast.2, bf16[6,3840,128]{2,1,0:T(8,128)(2,1)} %bitcast.3, bf16[6,8,32,128]{3,2,1,0:T(8,128)(2,1)} %go_hbm.1), custom_call_target="tpu_custom_call" | custom-call | flops 4499999744 | bytes 14000000 | tf_op jit(solution)/shard_map/attend/pallas_call | solution.py:208
  12.1 3.3 %collective-permute-start = (bf16[32,64,128]{2,1,0:T(8,128)(2,1)S(1)}, bf16[32,64,128]{2,1,0:T(8,128)(2,1)S(1)}, u32[]{:S(2)}, u32[]{:S(2)}) collective-permute-start(bf16[32,64,128]{2,1,0:T(8,128)(2,1)S(1)} %get-tuple-element.8), channel_id=1, source_target_pairs={{0,4},{4,0},{1,5},{5,1},{2,6},{6,2},{3,7},{7,3},{8,12},{12,8},{9,1... | collective-permute-start | bytes 1572872 | tf_op jit(solution)/shard_map/pair/ppermute | solution.py:356
  15.4 1.5 %collective-permute-done.peer_ref = bf16[32,64,128]{2,1,0:T(8,128)(2,1)S(1)} collective-permute-done((bf16[32,64,128]{2,1,0:T(8,128)(2,1)S(1)}, bf16[32,64,128]{2,1,0:T(8,128)(2,1)S(1)}, u32[]{:S(2)}, u32[]{:S(2)}) %collective-permute-start) | collective-permute-done | bytes 524320 | tf_op jit(solution)/shard_map/pair/ppermute | solution.py:356
  17.0 0.8 %pair.1 = bf16[32,56,128]{2,1,0:T(8,128)(2,1)S(1)} custom-call(bf16[32,64,128]{2,1,0:T(8,128)(2,1)S(1)} %collective-permute-done.peer_ref, f32[32,48,128]{2,1,0:T(8,128)S(1)} %get-tuple-element.9.own_ref, f32[32,8,128]{2,1,0:T(8,128)S(1)} %get-tuple-element.10.own_st_ref), custom_call_target="tpu_custom_call" | custom-call | flops 4000000 | bytes 2000000 | tf_op jit(solution)/shard_map/pair/pallas_call | solution.py:273
  17.7 24.7 %all_to_all.15.msg_ref = bf16[32,56,128]{2,1,0:T(8,128)(2,1)S(1)} all-to-all(bf16[32,56,128]{2,1,0:T(8,128)(2,1)S(1)} %pair.1), channel_id=1, replica_groups=mesh['z'=8,'y'=4,'c'=2,'x'=4] {'z','y'}, dimensions={0} | all-to-all | bytes 917504 | tf_op jit(solution)/shard_map/exchange/all_to_all | solution.py:359
  42.5 0.4 merge.1
  42.9 14.4 %all_to_all.16.msg_ref.own_ref = bf16[32,24,128]{2,1,0:T(8,128)(2,1)S(1)} all-to-all(bf16[32,24,128]{2,1,0:T(8,128)(2,1)S(1)} %merge.1), channel_id=1, replica_groups=mesh['z'=8,'y'=4,'c'=2,'x'=4] {'z','y'}, dimensions={0} | all-to-all | bytes 393216 | tf_op jit(solution)/shard_map/spread/all_to_all | solution.py:363
  57.3 3.2 %collective-permute-start.1 = (bf16[32,24,128]{2,1,0:T(8,128)(2,1)S(1)}, bf16[32,24,128]{2,1,0:T(8,128)(2,1)S(1)}, u32[]{:S(2)}, u32[]{:S(2)}) collective-permute-start(bf16[32,24,128]{2,1,0:T(8,128)(2,1)S(1)} %all_to_all.16.msg_ref.own_ref), channel_id=1, source_target_pairs={{0,4},{4,0},{1,5},{5,1},{2,6},{6,2},{3,7},{7,3},{8,12},{12,8},{9,1... | collective-permute-start | bytes 589832 | tf_op jit(solution)/shard_map/norm/ppermute | solution.py:365
  60.5 0.1 norm.2
  60.6 9.1 %all_to_all.17.sum_ref = f32[8,8,128]{2,1,0:T(8,128)S(1)} all-to-all(f32[8,8,128]{2,1,0:T(8,128)S(1)} %norm.2), channel_id=1, replica_groups=mesh['z'=8,'y'=4,'c'=2,'x'=4] {'c','x'}, dimensions={0} | all-to-all | bytes 65536 | tf_op jit(solution)/shard_map/norm/all_to_all | solution.py:366
  69.7 0.0 collective-permute-done.1.peer_ref
  69.7 0.8 %norm.3 = bf16[6,8,32,128]{3,2,1,0:T(8,128)(2,1)} custom-call(bf16[32,24,128]{2,1,0:T(8,128)(2,1)S(1)} %all_to_all.16.msg_ref.own_ref, bf16[32,24,128]{2,1,0:T(8,128)(2,1)S(1)} %collective-permute-done.1.peer_ref, f32[8,8,128]{2,1,0:T(8,128)S(1)} %all_to_all.17.sum_ref), custom_call_target="tpu_custom_call" | custom-call | flops 200000 | bytes 800000 | tf_op jit(solution)/shard_map/norm/pallas_call | solution.py:341
Async XLA Ops:
  12.1 4.9 %collective-permute-start = (bf16[32,64,128]{2,1,0:T(8,128)(2,1)S(1)}, bf16[32,64,128]{2,1,0:T(8,128)(2,1)S(1)}, u32[]{:S(2)}, u32[]{:S(2)}) collective-permute-start(bf16[32,64,128]{2,1,0:T(8,128)(2,1)S(1)} %get-tuple-element.8), channel_id=1, source_target_pairs={{0,4},{4,0},{1,5},{5,1},{2,6},{6,2},{3,7},{7,3},{8,12},{12,8},{9,1... | collective-permute-start | bytes 1572872 | tf_op jit(solution)/shard_map/pair/ppermute | solution.py:356
  57.3 12.4 %collective-permute-start.1 = (bf16[32,24,128]{2,1,0:T(8,128)(2,1)S(1)}, bf16[32,24,128]{2,1,0:T(8,128)(2,1)S(1)}, u32[]{:S(2)}, u32[]{:S(2)}) collective-permute-start(bf16[32,24,128]{2,1,0:T(8,128)(2,1)S(1)} %all_to_all.16.msg_ref.own_ref), channel_id=1, source_target_pairs={{0,4},{4,0},{1,5},{5,1},{2,6},{6,2},{3,7},{7,3},{8,12},{12,8},{9,1... | collective-permute-start | bytes 589832 | tf_op jit(solution)/shard_map/norm/ppermute | solution.py:365

commit v4 on v3

--- a/solution.py
+++ b/solution.py
@@ -34,13 +34,12 @@
 def attend(
     len_ref, q_hbm, k_hbm, v_hbm, go_hbm, peer_ref, own_ref, own_st_ref,
     q_buf, go_buf, k_buf, v_buf, s_a, s_b, s_c, g_a, g_b, g_c,
-    d_a, d_b, d_c, f_a, f_b, f_c, f_d, sems,
+    d_a, d_b, d_c, sems,
 ):
     core = lax.axis_index("c")
     count, rows = k_buf.shape[0], k_buf.shape[1]
     span = rows // 2
     chunks = -(-span // CHUNK)
-    flat = (f_a, f_b, f_c, f_d)
     start = ((lax.axis_index("z") * 4 + lax.axis_index("y")) * 2 + core) * span
 
     def sequence(j):
@@ -73,18 +72,14 @@
     def sides(x, reduce):
         return reduce(x, axis=0, keepdims=True)
 
-    def split(source, j, i, which):
+    def split(source, j, i):
         first, size = place(i)
-        scr = flat[which * 2 + i % 2]
-        scr[: 2 * size, :] = source[j, 2 * first : 2 * (first + size), :].astype(jnp.float32)
-        return jnp.concatenate(
-            [scr[pl.ds(side, size, stride=2), :].astype(jnp.bfloat16) for side in range(2)], axis=1
-        )
+        return source[j, 2 * first : 2 * (first + size), :].reshape(size, 2 * HD)
 
     def score_step(j, i, qt, gt, room, top):
         first, size = place(i)
         at = slice(first, first + size)
-        kd = split(k_buf, j, i, 0)
+        kd = split(k_buf, j, i)
         splits[j % 3][at, :] = kd
         s = jnp.dot(kd, qt, preferred_element_type=jnp.float32)
         tile_start = lax.broadcasted_iota(jnp.int32, (size // 8, 8, 128), 0) * 8
@@ -95,7 +90,7 @@
             half = jnp.where(visible, s[:, cols].reshape(size // 8, 8, 128), NEGATIVE)
             scores[j % 3][at, cols] = half.reshape(size, 128)
             peaks.append(jnp.max(half, axis=0))
-        vd = split(v_buf, j, i, 1)
+        vd = split(v_buf, j, i)
         probs[j % 3][at, :] = jnp.dot(vd, gt, preferred_element_type=jnp.float32)
         return jnp.maximum(top, jnp.concatenate(peaks, axis=1))
 
@@ -204,7 +199,6 @@
     )
     wide = pltpu.VMEM((span, 256), jnp.float32)
     slim = pltpu.VMEM((span, 256), jnp.bfloat16)
-    flat = pltpu.VMEM((2 * CHUNK, HD), jnp.float32)
     return pl.pallas_call(
         attend,
         in_specs=[pl.BlockSpec(memory_space=pltpu.SMEM), HBM, HBM, HBM, HBM],
@@ -219,7 +213,7 @@
             pltpu.VMEM(go.shape, jnp.bfloat16),
             pltpu.VMEM(k.shape, jnp.bfloat16),
             pltpu.VMEM(v.shape, jnp.bfloat16),
-            wide, wide, wide, wide, wide, wide, slim, slim, slim, flat, flat, flat, flat,
+            wide, wide, wide, wide, wide, wide, slim, slim, slim,
             pltpu.SemaphoreType.DMA((4 * count,)),
         ],
         compiler_params=pltpu.CompilerParams(vmem_limit_bytes=56 * MIB),

time: 70.7 us -> 69.6 us (0.984)
  Pallas kernels: 14.2 us -> 13.1 us
    pallas_call x1, Pallas kernels: 12.1 us -> 10.9 us  [attend_call(): pl.pallas_call(attend, in_specs=[pl.BlockSpec(memory_space=pltpu.SMEM), H...]
where the time goes in v4:
time: 69.6 us; the launch traced here: 69.4 us
  blocking collectives  48.3 us (69%)
  Pallas kernels  13.1 us (19%)
  starting transfers between devices  6.48 us (9%)
  waiting for transfers between devices  1.54 us (2%)
    all_to_all x2, blocking collectives, local(): msg = lax.all_to_all(msg, ('z', 'y'), 0, 0)  39.1 us
    pallas_call x1, Pallas kernels, attend_call(): pl.pallas_call(attend, in_specs=[pl.BlockSpec(memory_space=pltpu.SMEM), H...  10.9 us
    all_to_all x1, blocking collectives, local(): sums = lax.all_to_all(squares_call(msg), ('c', 'x'), 0, 0)  9.13 us
    ppermute x1, starting transfers between devices, local(): peer = lax.ppermute(peer, 'c', swap)  3.33 us
    ppermute x1, starting transfers between devices, local(): other = lax.ppermute(msg, 'c', swap)  3.15 us
    ppermute x1, waiting for transfers between devices, local(): peer = lax.ppermute(peer, 'c', swap)  1.54 us
  transfers between devices with their start and end apart: 2, of which 1 were waited for; matrix products, arithmetic and copies ran while one was open for 0% of the time, Pallas kernels for 0%

profile of v4, /device:TPU:1, one launch (start us, length us, event | category | flops | bytes accessed | tf_op | source)
XLA Modules:
  0.0 69.4 jit_solution(10122114575423508292)
XLA Ops:
  0.0 10.9 %attend.1 = (bf16[32,64,128]{2,1,0:T(8,128)(2,1)S(1)}, f32[32,48,128]{2,1,0:T(8,128)S(1)}, f32[32,8,128]{2,1,0:T(8,128)S(1)}) custom-call(s32[6]{0:T(128)} %len_ref.1, bf16[6,8,32,128]{3,2,1,0:T(8,128)(2,1)} %q_hbm.1, bf16[6,3840,128]{2,1,0:T(8,128)(2,1)} %bitcast.2, bf16[6,3840,128]{2,1,0:T(8,128)(2,1)} %bitcast.3, bf16[6,8,32,128]{3,2,1,0:T(8,128)(2,1)} %go_hbm.1), custom_call_target="tpu_custom_call" | custom-call | flops 4499999744 | bytes 14000000 | tf_op jit(solution)/shard_map/attend/pallas_call | solution.py:202
  10.9 3.3 %collective-permute-start = (bf16[32,64,128]{2,1,0:T(8,128)(2,1)S(1)}, bf16[32,64,128]{2,1,0:T(8,128)(2,1)S(1)}, u32[]{:S(2)}, u32[]{:S(2)}) collective-permute-start(bf16[32,64,128]{2,1,0:T(8,128)(2,1)S(1)} %get-tuple-element.8), channel_id=1, source_target_pairs={{0,4},{4,0},{1,5},{5,1},{2,6},{6,2},{3,7},{7,3},{8,12},{12,8},{9,1... | collective-permute-start | bytes 1572872 | tf_op jit(solution)/shard_map/pair/ppermute | solution.py:350
  14.3 1.5 %collective-permute-done.peer_ref = bf16[32,64,128]{2,1,0:T(8,128)(2,1)S(1)} collective-permute-done((bf16[32,64,128]{2,1,0:T(8,128)(2,1)S(1)}, bf16[32,64,128]{2,1,0:T(8,128)(2,1)S(1)}, u32[]{:S(2)}, u32[]{:S(2)}) %collective-permute-start) | collective-permute-done | bytes 524320 | tf_op jit(solution)/shard_map/pair/ppermute | solution.py:350
  15.8 0.8 %pair.1 = bf16[32,56,128]{2,1,0:T(8,128)(2,1)S(1)} custom-call(bf16[32,64,128]{2,1,0:T(8,128)(2,1)S(1)} %collective-permute-done.peer_ref, f32[32,48,128]{2,1,0:T(8,128)S(1)} %get-tuple-element.9.own_ref, f32[32,8,128]{2,1,0:T(8,128)S(1)} %get-tuple-element.10.own_st_ref), custom_call_target="tpu_custom_call" | custom-call | flops 4000000 | bytes 2000000 | tf_op jit(solution)/shard_map/pair/pallas_call | solution.py:267
  16.6 24.7 %all_to_all.15.msg_ref = bf16[32,56,128]{2,1,0:T(8,128)(2,1)S(1)} all-to-all(bf16[32,56,128]{2,1,0:T(8,128)(2,1)S(1)} %pair.1), channel_id=1, replica_groups=mesh['z'=8,'y'=4,'c'=2,'x'=4] {'z','y'}, dimensions={0} | all-to-all | bytes 917504 | tf_op jit(solution)/shard_map/exchange/all_to_all | solution.py:353
  41.3 0.4 merge.1
  41.7 14.4 %all_to_all.16.msg_ref.own_ref = bf16[32,24,128]{2,1,0:T(8,128)(2,1)S(1)} all-to-all(bf16[32,24,128]{2,1,0:T(8,128)(2,1)S(1)} %merge.1), channel_id=1, replica_groups=mesh['z'=8,'y'=4,'c'=2,'x'=4] {'z','y'}, dimensions={0} | all-to-all | bytes 393216 | tf_op jit(solution)/shard_map/spread/all_to_all | solution.py:357
  56.1 3.2 %collective-permute-start.1 = (bf16[32,24,128]{2,1,0:T(8,128)(2,1)S(1)}, bf16[32,24,128]{2,1,0:T(8,128)(2,1)S(1)}, u32[]{:S(2)}, u32[]{:S(2)}) collective-permute-start(bf16[32,24,128]{2,1,0:T(8,128)(2,1)S(1)} %all_to_all.16.msg_ref.own_ref), channel_id=1, source_target_pairs={{0,4},{4,0},{1,5},{5,1},{2,6},{6,2},{3,7},{7,3},{8,12},{12,8},{9,1... | collective-permute-start | bytes 589832 | tf_op jit(solution)/shard_map/norm/ppermute | solution.py:359
  59.3 0.1 norm.2
  59.4 9.1 %all_to_all.17.sum_ref = f32[8,8,128]{2,1,0:T(8,128)S(1)} all-to-all(f32[8,8,128]{2,1,0:T(8,128)S(1)} %norm.2), channel_id=1, replica_groups=mesh['z'=8,'y'=4,'c'=2,'x'=4] {'c','x'}, dimensions={0} | all-to-all | bytes 65536 | tf_op jit(solution)/shard_map/norm/all_to_all | solution.py:360
  68.5 0.0 collective-permute-done.1.peer_ref
  68.5 0.8 %norm.3 = bf16[6,8,32,128]{3,2,1,0:T(8,128)(2,1)} custom-call(bf16[32,24,128]{2,1,0:T(8,128)(2,1)S(1)} %all_to_all.16.msg_ref.own_ref, bf16[32,24,128]{2,1,0:T(8,128)(2,1)S(1)} %collective-permute-done.1.peer_ref, f32[8,8,128]{2,1,0:T(8,128)S(1)} %all_to_all.17.sum_ref), custom_call_target="tpu_custom_call" | custom-call | flops 200000 | bytes 800000 | tf_op jit(solution)/shard_map/norm/pallas_call | solution.py:335
Async XLA Ops:
  10.9 4.9 %collective-permute-start = (bf16[32,64,128]{2,1,0:T(8,128)(2,1)S(1)}, bf16[32,64,128]{2,1,0:T(8,128)(2,1)S(1)}, u32[]{:S(2)}, u32[]{:S(2)}) collective-permute-start(bf16[32,64,128]{2,1,0:T(8,128)(2,1)S(1)} %get-tuple-element.8), channel_id=1, source_target_pairs={{0,4},{4,0},{1,5},{5,1},{2,6},{6,2},{3,7},{7,3},{8,12},{12,8},{9,1... | collective-permute-start | bytes 1572872 | tf_op jit(solution)/shard_map/pair/ppermute | solution.py:350
  56.1 12.4 %collective-permute-start.1 = (bf16[32,24,128]{2,1,0:T(8,128)(2,1)S(1)}, bf16[32,24,128]{2,1,0:T(8,128)(2,1)S(1)}, u32[]{:S(2)}, u32[]{:S(2)}) collective-permute-start(bf16[32,24,128]{2,1,0:T(8,128)(2,1)S(1)} %all_to_all.16.msg_ref.own_ref), channel_id=1, source_target_pairs={{0,4},{4,0},{1,5},{5,1},{2,6},{6,2},{3,7},{7,3},{8,12},{12,8},{9,1... | collective-permute-start | bytes 589832 | tf_op jit(solution)/shard_map/norm/ppermute | solution.py:359

commit v5 on v4

--- a/solution.py
+++ b/solution.py
@@ -19,6 +19,7 @@
 SCALE = 1.0 / math.sqrt(HD)
 SCALE2 = SCALE * math.log2(math.e)
 CHUNK = 256
+SPLIT = 512
 PARTS = 3
 SLOT = 56
 MIB = 1024 * 1024
@@ -54,9 +55,18 @@
             pltpu.make_async_copy(source.at[sequence(j)], target.at[j], sems.at[base + j]) for j in range(count)
         ]
 
+    def first_part(source, target, half, sem):
+        begin, end = (0, SPLIT) if half == 0 else (SPLIT, span)
+        at = pl.ds(2 * begin, 2 * (end - begin))
+        return pltpu.make_async_copy(source.at[sequence(0), at], target.at[0, at], sems.at[sem])
+
     keys, values = whole(k_hbm, k_buf, 0), whole(v_hbm, v_buf, count)
     small = list(zip(whole(q_hbm, q_buf, 2 * count), whole(go_hbm, go_buf, 3 * count)))
-    for j in range(count):
+    early = [first_part(k_hbm, k_buf, 0, 0), first_part(v_hbm, v_buf, 0, count)]
+    late = [first_part(k_hbm, k_buf, 1, 4 * count), first_part(v_hbm, v_buf, 1, 4 * count + 1)]
+    for copy in (*small[0], *early, *late):
+        copy.start()
+    for j in range(1, count):
         for copy in (small[j][0], keys[j], small[j][1], values[j]):
             copy.start()
 
@@ -120,7 +130,7 @@
 
     def prepare(j):
         seq = sequence(j)
-        for copy in (*small[j], keys[j], values[j]):
+        for copy in (*small[j], *(early if j == 0 else (keys[j], values[j]))):
             copy.wait()
         return turned(q_buf[j]), turned(go_buf[j]), len_ref[seq] - QT - start
 
@@ -163,6 +173,9 @@
         if 0 <= third:
             acc = [jnp.zeros((128, 256), jnp.float32)] * 2
         for i in range(chunks):
+            if first == 0 and i * CHUNK == SPLIT:
+                for copy in late:
+                    copy.wait()
             if 0 <= third:
                 acc = term_step(third, i, stats[third][2], acc)
             if first < count:
@@ -214,7 +227,7 @@
             pltpu.VMEM(k.shape, jnp.bfloat16),
             pltpu.VMEM(v.shape, jnp.bfloat16),
             wide, wide, wide, wide, wide, wide, slim, slim, slim,
-            pltpu.SemaphoreType.DMA((4 * count,)),
+            pltpu.SemaphoreType.DMA((4 * count + 2,)),
         ],
         compiler_params=pltpu.CompilerParams(vmem_limit_bytes=56 * MIB),
         cost_estimate=pl.CostEstimate(flops=4_500_000_000, bytes_accessed=14_000_000, transcendentals=3_000_000),
@@ -321,22 +334,29 @@
     )(msg)
 
 
-def finish(own_ref, peer_ref, sum_ref, out_ref):
+def finish(own_ref, peer_ref, sum_ref, out_hbm, rows_buf, sems):
     core = lax.axis_index("c")
     squares = jnp.sum(sum_ref[...], axis=0)[:1]
     factor = 1.0 / jnp.sqrt(squares / (B * QT * HQ * HD) + EPSILON)
+    copies = []
     for ref, odd in ((own_ref, core), (peer_ref, 1 - core)):
         rows = ref[...].astype(jnp.float32) * factor
         for part in range(PARTS):
-            out_ref[2 * part + odd] = rows[:, part * 8 : part * 8 + 8].reshape(QT, 32, HD).astype(jnp.bfloat16)
+            slot = len(copies)
+            rows_buf[slot] = rows[:, part * 8 : part * 8 + 8].reshape(QT, 32, HD).astype(jnp.bfloat16)
+            copies.append(pltpu.make_async_copy(rows_buf.at[slot], out_hbm.at[2 * part + odd], sems.at[slot]))
+            copies[slot].start()
+    for copy in copies:
+        copy.wait()
 
 
 def finish_call(own, peer, sums):
     return pl.pallas_call(
         finish,
         in_specs=[VMEM] * 3,
-        out_specs=VMEM,
+        out_specs=HBM,
         out_shape=jax.ShapeDtypeStruct((B, QT, 32, HD), jnp.bfloat16),
+        scratch_shapes=[pltpu.VMEM((B, QT, 32, HD), jnp.bfloat16), pltpu.SemaphoreType.DMA((B,))],
         compiler_params=pltpu.CompilerParams(vmem_limit_bytes=16 * MIB),
         cost_estimate=pl.CostEstimate(flops=200_000, bytes_accessed=800_000, transcendentals=0),
     )(own, peer, sums)

time: 69.6 us -> 69.5 us (level)
  no operation moved by 1% of the time
where the time goes in v5:
time: 69.5 us; the launch traced here: 69.3 us
  blocking collectives  48.3 us (69%)
  Pallas kernels  13 us (19%)
  starting transfers between devices  6.48 us (9%)
  waiting for transfers between devices  1.54 us (2%)
    all_to_all x2, blocking collectives, local(): msg = lax.all_to_all(msg, ('z', 'y'), 0, 0)  39.1 us
    pallas_call x1, Pallas kernels, attend_call(): pl.pallas_call(attend, in_specs=[pl.BlockSpec(memory_space=pltpu.SMEM), H...  10.9 us
    all_to_all x1, blocking collectives, local(): sums = lax.all_to_all(squares_call(msg), ('c', 'x'), 0, 0)  9.11 us
    ppermute x1, starting transfers between devices, local(): peer = lax.ppermute(peer, 'c', swap)  3.33 us
    ppermute x1, starting transfers between devices, local(): other = lax.ppermute(msg, 'c', swap)  3.15 us
    ppermute x1, waiting for transfers between devices, local(): peer = lax.ppermute(peer, 'c', swap)  1.54 us
  transfers between devices with their start and end apart: 2, of which 1 were waited for; matrix products, arithmetic and copies ran while one was open for 0% of the time, Pallas kernels for 0%

profile of v5, /device:TPU:1, one launch (start us, length us, event | category | flops | bytes accessed | tf_op | source)
XLA Modules:
  0.0 69.3 jit_solution(11380400430079415045)
XLA Ops:
  0.0 10.9 %attend.1 = (bf16[32,64,128]{2,1,0:T(8,128)(2,1)S(1)}, f32[32,48,128]{2,1,0:T(8,128)S(1)}, f32[32,8,128]{2,1,0:T(8,128)S(1)}) custom-call(s32[6]{0:T(128)} %len_ref.1, bf16[6,8,32,128]{3,2,1,0:T(8,128)(2,1)} %q_hbm.1, bf16[6,3840,128]{2,1,0:T(8,128)(2,1)} %bitcast.2, bf16[6,3840,128]{2,1,0:T(8,128)(2,1)} %bitcast.3, bf16[6,8,32,128]{3,2,1,0:T(8,128)(2,1)} %go_hbm.1), custom_call_target="tpu_custom_call" | custom-call | flops 4499999744 | bytes 14000000 | tf_op jit(solution)/shard_map/attend/pallas_call | solution.py:215
  10.9 3.3 %collective-permute-start = (bf16[32,64,128]{2,1,0:T(8,128)(2,1)S(1)}, bf16[32,64,128]{2,1,0:T(8,128)(2,1)S(1)}, u32[]{:S(2)}, u32[]{:S(2)}) collective-permute-start(bf16[32,64,128]{2,1,0:T(8,128)(2,1)S(1)} %get-tuple-element.8), channel_id=1, source_target_pairs={{0,4},{4,0},{1,5},{5,1},{2,6},{6,2},{3,7},{7,3},{8,12},{12,8},{9,1... | collective-permute-start | bytes 1572872 | tf_op jit(solution)/shard_map/pair/ppermute | solution.py:370
  14.2 1.5 %collective-permute-done.peer_ref = bf16[32,64,128]{2,1,0:T(8,128)(2,1)S(1)} collective-permute-done((bf16[32,64,128]{2,1,0:T(8,128)(2,1)S(1)}, bf16[32,64,128]{2,1,0:T(8,128)(2,1)S(1)}, u32[]{:S(2)}, u32[]{:S(2)}) %collective-permute-start) | collective-permute-done | bytes 524320 | tf_op jit(solution)/shard_map/pair/ppermute | solution.py:370
  15.7 0.8 %pair.1 = bf16[32,56,128]{2,1,0:T(8,128)(2,1)S(1)} custom-call(bf16[32,64,128]{2,1,0:T(8,128)(2,1)S(1)} %collective-permute-done.peer_ref, f32[32,48,128]{2,1,0:T(8,128)S(1)} %get-tuple-element.9.own_ref, f32[32,8,128]{2,1,0:T(8,128)S(1)} %get-tuple-element.10.own_st_ref), custom_call_target="tpu_custom_call" | custom-call | flops 4000000 | bytes 2000000 | tf_op jit(solution)/shard_map/pair/pallas_call | solution.py:280
  16.5 24.7 %all_to_all.15.msg_ref = bf16[32,56,128]{2,1,0:T(8,128)(2,1)S(1)} all-to-all(bf16[32,56,128]{2,1,0:T(8,128)(2,1)S(1)} %pair.1), channel_id=1, replica_groups=mesh['z'=8,'y'=4,'c'=2,'x'=4] {'z','y'}, dimensions={0} | all-to-all | bytes 917504 | tf_op jit(solution)/shard_map/exchange/all_to_all | solution.py:373
  41.2 0.4 merge.1
  41.7 14.4 %all_to_all.16.msg_ref.own_ref = bf16[32,24,128]{2,1,0:T(8,128)(2,1)S(1)} all-to-all(bf16[32,24,128]{2,1,0:T(8,128)(2,1)S(1)} %merge.1), channel_id=1, replica_groups=mesh['z'=8,'y'=4,'c'=2,'x'=4] {'z','y'}, dimensions={0} | all-to-all | bytes 393216 | tf_op jit(solution)/shard_map/spread/all_to_all | solution.py:377
  56.1 3.2 %collective-permute-start.1 = (bf16[32,24,128]{2,1,0:T(8,128)(2,1)S(1)}, bf16[32,24,128]{2,1,0:T(8,128)(2,1)S(1)}, u32[]{:S(2)}, u32[]{:S(2)}) collective-permute-start(bf16[32,24,128]{2,1,0:T(8,128)(2,1)S(1)} %all_to_all.16.msg_ref.own_ref), channel_id=1, source_target_pairs={{0,4},{4,0},{1,5},{5,1},{2,6},{6,2},{3,7},{7,3},{8,12},{12,8},{9,1... | collective-permute-start | bytes 589832 | tf_op jit(solution)/shard_map/norm/ppermute | solution.py:379
  59.2 0.1 norm.2
  59.3 9.1 %all_to_all.17.sum_ref = f32[8,8,128]{2,1,0:T(8,128)S(1)} all-to-all(f32[8,8,128]{2,1,0:T(8,128)S(1)} %norm.2), channel_id=1, replica_groups=mesh['z'=8,'y'=4,'c'=2,'x'=4] {'c','x'}, dimensions={0} | all-to-all | bytes 65536 | tf_op jit(solution)/shard_map/norm/all_to_all | solution.py:380
  68.5 0.0 collective-permute-done.1.peer_ref
  68.5 0.8 %norm.3 = bf16[6,8,32,128]{3,2,1,0:T(8,128)(2,1)} custom-call(bf16[32,24,128]{2,1,0:T(8,128)(2,1)S(1)} %all_to_all.16.msg_ref.own_ref, bf16[32,24,128]{2,1,0:T(8,128)(2,1)S(1)} %collective-permute-done.1.peer_ref, f32[8,8,128]{2,1,0:T(8,128)S(1)} %all_to_all.17.sum_ref), custom_call_target="tpu_custom_call" | custom-call | flops 200000 | bytes 800000 | tf_op jit(solution)/shard_map/norm/pallas_call | solution.py:354
Async XLA Ops:
  10.9 4.9 %collective-permute-start = (bf16[32,64,128]{2,1,0:T(8,128)(2,1)S(1)}, bf16[32,64,128]{2,1,0:T(8,128)(2,1)S(1)}, u32[]{:S(2)}, u32[]{:S(2)}) collective-permute-start(bf16[32,64,128]{2,1,0:T(8,128)(2,1)S(1)} %get-tuple-element.8), channel_id=1, source_target_pairs={{0,4},{4,0},{1,5},{5,1},{2,6},{6,2},{3,7},{7,3},{8,12},{12,8},{9,1... | collective-permute-start | bytes 1572872 | tf_op jit(solution)/shard_map/pair/ppermute | solution.py:370
  56.1 12.4 %collective-permute-start.1 = (bf16[32,24,128]{2,1,0:T(8,128)(2,1)S(1)}, bf16[32,24,128]{2,1,0:T(8,128)(2,1)S(1)}, u32[]{:S(2)}, u32[]{:S(2)}) collective-permute-start(bf16[32,24,128]{2,1,0:T(8,128)(2,1)S(1)} %all_to_all.16.msg_ref.own_ref), channel_id=1, source_target_pairs={{0,4},{4,0},{1,5},{5,1},{2,6},{6,2},{3,7},{7,3},{8,12},{12,8},{9,1... | collective-permute-start | bytes 589832 | tf_op jit(solution)/shard_map/norm/ppermute | solution.py:379
